TPU v7x, 32 devices: a whole 2x2x4 slice. The times are simulated.
32 devices in a mesh: img: 16 (over z, y, x), pix: 2 (over core).
Axes of the slice: x: 2, y: 2, z: 4, core: 2. Of those that a mesh axis runs over, the one named last changes fastest.
Arguments:
- images: bfloat16 [4096, 16384], P('img', 'pix'), may hold values from -100 to 100
- references: bfloat16 [1536, 16384], P('img', 'pix'), may hold values from -6 to 6
- cycle_mask: int32 [16384], P('pix'), may hold values from 0 to 1, as said below
- view_class: int32 [1536], replicated, may hold values from 0 to 95, as said below
Outputs:
- view_sums: float32 [1536, 16384], P('img', 'pix')
- class_share: float32 [96], replicated
- image_evidence: float32 [4096], P(('img', 'pix'))
Inputs may be any that keep to these rules, and one draw needn't show every extreme that they name: `cycle_mask`: only pixels whose distance from the image centre lies between an inner radius and 64 are 1; some of them are left out as defective, never those in even columns, so the cycle is never empty. `view_class`: every class is named by exactly 16 views.
All inputs are finite; a program needn't handle non-finite values.
Results may differ from a plain program's by a relative error of at most 0.0023.
Values may be sent and summed in bfloat16 or wider, within the bound.
A program may use at most 128 MiB of HBM per device.

v0:
```python
import jax
import jax.numpy as jnp
from jax import lax
from jax.sharding import PartitionSpec as P

SIDE = 128
NCLS = 96


EPSILON = 1e-05


def softmax_rows(scores):
    row_max = jnp.max(scores, 1, keepdims=True)
    log_total = row_max[:, 0] + jnp.log(jnp.sum(jnp.exp(scores - row_max), 1))
    evidence = log_total - jnp.mean(scores, 1)
    posterior = jnp.exp(scores - log_total[:, None]).astype(jnp.bfloat16)
    return (posterior, evidence)


def on_device(images, references, cycle_mask, view_class):
    total_images = images.shape[0] * lax.axis_size("img")
    widened = images.astype(jnp.float32)
    col_sum, col_sq = lax.psum((jnp.sum(widened, 0), jnp.sum(widened * widened, 0)), "img")
    pix_mean = col_sum / total_images
    pix_std = jnp.sqrt(col_sq / total_images - pix_mean * pix_mean + EPSILON)
    whitened = (widened - pix_mean) / pix_std
    cycle_weight = cycle_mask.astype(jnp.float32)
    cycle_sum, cycle_sq, cycle_count = lax.psum(
        (
            jnp.sum(whitened * cycle_weight, 1),
            jnp.sum(whitened * whitened * cycle_weight, 1),
            jnp.sum(cycle_weight),
        ),
        "pix",
    )
    bg_mean = cycle_sum / cycle_count
    bg_std = jnp.sqrt(cycle_sq / cycle_count - bg_mean * bg_mean + EPSILON)
    normed = ((whitened - bg_mean[:, None]) / bg_std[:, None]).astype(jnp.bfloat16)
    ref_piece = lax.all_gather(references, "img", axis=0, tiled=True)
    ref_energy = jnp.sum(jnp.square(ref_piece.astype(jnp.float32)), 1)
    raw = lax.dot_general(
        normed, ref_piece, (((1,), (1,)), ((), ())), preferred_element_type=jnp.float32
    )
    partial_value = raw - 0.5 * ref_energy[None, :]
    factor = 4.0 / SIDE
    share_rows = images.shape[0] // lax.axis_size("pix")
    scores = lax.psum(partial_value, "pix") * factor
    posterior, full_evidence = softmax_rows(scores)
    evidence = lax.dynamic_slice_in_dim(
        full_evidence, lax.axis_index("pix") * share_rows, share_rows
    )
    view_sums = lax.psum_scatter(
        lax.dot_general(
            posterior, normed, (((0,), (0,)), ((), ())), preferred_element_type=jnp.float32
        ),
        "img",
        scatter_dimension=0,
        tiled=True,
    )
    class_mass = jnp.sum(posterior, 0, dtype=jnp.float32)
    onehot = (view_class[:, None] == jnp.arange(NCLS, dtype=jnp.int32)[None, :]).astype(jnp.float32)
    class_local = jnp.dot(class_mass, onehot, precision=lax.Precision.HIGHEST)
    class_total = lax.psum(class_local, "img")
    return (view_sums, class_total * (NCLS / total_images), evidence)


def solution(mesh):
    in_specs = (P("img", "pix"), P("img", "pix"), P("pix"), P())
    out_specs = (P("img", "pix"), P(), P(("img", "pix")))
    return jax.shard_map(
        on_device, mesh=mesh, in_specs=in_specs, out_specs=out_specs, check_vma=False
    )
```

profile of v0, /device:TPU:0, one launch (start us, length us, event | category | flops | bytes accessed | tf_op | source)
XLA Modules:
  0.0 1170.2 jit_solution(7877020838066826043)
XLA Ops:
  7.2 0.0 copy-start.1
  7.2 0.0 all-reduce.7.cloned.1.call-start
  7.2 4.0 convert_reduce_fusion
  11.2 0.0 all-reduce.7.cloned.1.call-update
  11.2 0.0 all-gather.2.cloned.1.call-start
  11.3 0.7 all-gather.2.cloned.1.call-update
  12.0 0.0 all-reduce.5.cloned.1.call-start
  12.0 0.0 copy-done.1
  12.1 0.6 convert_reduce_fusion.2
  12.7 106.7 %all-reduce.7.cloned.1.call-done = (f32[8192]{0:T(1024)}, f32[8192]{0:T(1024)}) async-done(((f32[8192]{0:T(1024)}, f32[8192]{0:T(1024)}), (f32[8192]{0:T(1024)}, f32[8192]{0:T(1024)})) %all-reduce.7.cloned.1.call-update) | async-done | bytes 65552 | tf_op jit(solution)/shard_map/psum | solution.py:24
  119.4 0.8 broadcast_multiply_fusion
  120.1 4.2 multiply_reduce_fusion.1
  124.4 3.1 all-reduce.1
  127.5 0.7 add_sqrt_fusion.1
  128.1 264.7 %all-gather.2.cloned.1.call-done = bf16[1536,8192]{1,0:T(8,128)(2,1)} async-done(((bf16[96,8192]{1,0:T(8,128)(2,1)}), bf16[1536,8192]{1,0:T(8,128)(2,1)}) %all-gather.2.cloned.1.call-update) | async-done | bytes 25165840 | tf_op jit(solution)/shard_map/all_gather | solution.py:40
  392.8 10.3 multiply_reduce_fusion
  403.2 14.7 %convolution_subtract_fusion = f32[256,1536]{1,0:T(8,128)} fusion(bf16[1536,8192]{1,0:T(8,128)(2,1)} %all-gather.2.cloned.1.call-done, f32[1536]{0:T(1024)S(1)} %broadcast_multiply_fusion.1, f32[256]{0:T(256)S(1)} %get-tuple-element.14, f32[256]{0:T(256)S(1)} %get-tuple-element.15, f32[8192]{0:T(1024)S(1)} %get-tuple-element.17, ...), kind=kOutput, calls=%fused_computation.9 | convolution fusion | flops 6455427072 | bytes 31006720 | tf_op jit(solution)/shard_map/dot_general | solution.py:42
  417.9 0.0 all-reduce.5.cloned.1.call-update
  417.9 0.2 reduce-scatter.2.cloned.1.call-start
  418.1 18.5 %all-reduce.5.cloned.1.call-done = f32[256,1536]{1,0:T(8,128)} async-done(((f32[256,1536]{1,0:T(8,128)}), f32[256,1536]{1,0:T(8,128)}) %all-reduce.5.cloned.1.call-update) | async-done | bytes 1572880 | tf_op jit(solution)/shard_map/psum | solution.py:48
  436.6 1.6 multiply_reduce_fusion.4
  438.2 1.8 exponential_reduce_fusion
  440.0 21.7 %fusion.3 = f32[1536,8192]{1,0:T(8,128)} fusion(f32[256,1536]{1,0:T(8,128)} %all-reduce.5.cloned.1.call-done, f32[256]{0:T(256)S(1)} %log_add_fusion, f32[256]{0:T(256)S(1)} %get-tuple-element.14, f32[256]{0:T(256)S(1)} %get-tuple-element.15, f32[8192]{0:T(1024)S(1)} %get-tuple-element.17, f32[8192]{0:T(1024)S(1)} %get-tuple-element.16, ...), kind=kOutput, calls=%fused_computation.28 | convolution fusion | flops 6456213504 | bytes 56167424 | tf_op jit(solution)/shard_map/dot_general | solution.py:54
  461.7 0.0 copy-start
  461.7 0.0 copy-start.2
  461.7 0.0 reduce-scatter.2.cloned.1.call-update
  461.8 1.4 copy-done
  463.1 0.4 multiply_reduce_fusion.3
  463.5 0.6 dynamic_slice.3
  464.1 0.0 copy-done.2
  464.1 0.5 convolution_bitcast_fusion
  464.6 44.0 %psum.55 = f32[96]{0:T(128)S(1)} all-reduce(f32[96]{0:T(128)S(1)} %convolution_bitcast_fusion), channel_id=1, replica_groups=mesh['img'=16,'pix'=2] {'img'}, use_global_device_ids=true, to_apply=%region_16.0 | all-reduce | flops 96 | bytes 768 | tf_op jit(solution)/shard_map/psum | solution.py:64
  508.7 0.5 broadcast_multiply_fusion.2
  509.2 654.5 %reduce-scatter.2.cloned.1.call-done = f32[96,8192]{1,0:T(8,128)} async-done(((f32[1536,8192]{1,0:T(8,128)}), f32[96,8192]{1,0:T(8,128)}) %reduce-scatter.2.cloned.1.call-update) | async-done | bytes 3145744 | tf_op jit(solution)/shard_map/reduce_scatter | solution.py:53
  (5 shorter events, 0.0 us)
Async XLA Ops:
  7.2 4.9 copy-start.1
  7.2 112.2 %all-reduce.7.cloned.1.call-start = ((), (), s32[]{:S(2)}) async-start(), calls=%async_computation.4 | async-start | bytes 131072 | tf_op jit(solution)/shard_map/psum | solution.py:24
  11.2 381.6 %all-gather.2.cloned.1.call-start = ((), (), s32[]{:S(2)}) async-start(), calls=%async_computation.1 | async-start | bytes 26738688 | tf_op jit(solution)/shard_map/all_gather | solution.py:40
  12.0 424.6 %all-reduce.5.cloned.1.call-start = ((), (), s32[]{:S(2)}) async-start(), calls=%async_computation.2 | async-start | bytes 3145728 | tf_op jit(solution)/shard_map/psum | solution.py:48
  417.9 745.8 %reduce-scatter.2.cloned.1.call-start = ((), (), s32[]{:S(2)}) async-start(), calls=%async_computation.3 | async-start | bytes 53477376 | tf_op jit(solution)/shard_map/reduce_scatter | solution.py:53
  461.7 1.4 copy-start
  461.7 2.4 copy-start.2
Sparse Core Ops, SparseCore 0:
  14.2 105.1 all-reduce.6
  122.5 270.2 all-gather.1
  418.0 18.5 all-reduce.4
  461.9 701.7 reduce-scatter.1
where the time goes:
time: 1170 us
  waiting for transfers between devices  1050 us (90%)
  blocking collectives  47.1 us (4%)
  matrix products  36.9 us (3%)
  other arithmetic  24.9 us (2%)
  between operations  13.8 us (1%)
    reduce_scatter x1, waiting for transfers between devices, on_device(): lax.psum_scatter(lax.dot_general(posterior, normed, (((0,), (0,)), ((), (...  654 us
    all_gather x1, waiting for transfers between devices, on_device(): ref_piece = lax.all_gather(references, 'img', axis=0, tiled=True)  265 us
    psum x1, waiting for transfers between devices, on_device(): lax.psum((jnp.sum(widened, 0), jnp.sum(widened * widened, 0)), 'img')  107 us
    psum x1, blocking collectives, on_device(): class_total = lax.psum(class_local, 'img')  44 us
  transfers between devices with their start and end apart: 4, of which 4 were waited for; matrix products, arithmetic and copies ran while one was open for 1% of the time, Pallas kernels for 0%

commit v1 on v0

v1 whole, which is shorter than its diff:
```python
import functools

import jax
import jax.numpy as jnp
from jax import lax
from jax.experimental import pallas as pl
from jax.experimental.pallas import tpu as pltpu
from jax.sharding import PartitionSpec as P

SIDE = 128
NCLS = 96
EPSILON = 1e-05
MESH = pl.DeviceIdType.MESH

PIXEL_BIT = 4
VIEW_BIT = 2


def image_bits(n):
    return [b for b in (1, *reversed([2**j for j in range(3, 20) if 2**j < n]))]


def bit(index, value):
    return (index // value) % 2


def flip(index, value):
    return index + value * (1 - 2 * bit(index, value))


def greet(partners):
    barrier = pltpu.get_barrier_semaphore()
    for p in partners:
        pl.semaphore_signal(barrier, inc=1, device_id={"img": p}, device_id_type=MESH)
    pl.semaphore_wait(barrier, len(partners))


def gather_kernel(n, chunks, images, refs, img_all, ref_all, lsem, isend, irecv, rsend, rrecv):
    d = lax.axis_index("img")
    bits = image_bits(n)
    nr = len(bits)
    k, c = bit(d, PIXEL_BIT), bit(d, VIEW_BIT)
    kp, cp = flip(d, PIXEL_BIT), flip(d, VIEW_BIT)
    rows, cols = images.shape
    q = cols // 2
    mine = pl.ds(pl.multiple_of(k * q, 128), q)
    theirs = pl.ds(pl.multiple_of((1 - k) * q, 128), q)
    weights = [2 ** (nr - j) for j in range(nr)]
    slot = k
    for b, w in zip(bits, weights):
        slot = slot + w * bit(d, b)

    greet([kp, cp] + [flip(d, b) for b in bits])

    def remote(src, dst, ssem, rsem, partner):
        cp_ = pltpu.make_async_remote_copy(
            src_ref=src, dst_ref=dst, send_sem=ssem, recv_sem=rsem,
            device_id={"img": partner}, device_id_type=MESH)
        cp_.start()
        return cp_

    step = rows // chunks
    own = 2 * c + k
    other = 2 * c + 1 - k
    ref_copies = []

    def send_ref(src, s, partner):
        i = len(ref_copies)
        ref_copies.append(remote(src, ref_all.at[s], rsend.at[i], rrecv.at[i], partner))
        return ref_copies[-1]

    img_copies = []

    def send_img(src, dst, partner):
        i = len(img_copies)
        img_copies.append(remote(src, dst, isend.at[i], irecv.at[i], partner))
        return img_copies[-1]

    order = list(reversed(list(zip(bits, weights))))
    pair_ref = send_ref(refs.at[:, theirs], slot, kp)
    own_refs = refs.at[:, mine]
    stage = [[] for _ in order]
    for j, (b, w) in enumerate(order):
        stage[j].append((send_ref(own_refs, slot, flip(d, b)), slot))
    img_k = []
    for i in range(chunks):
        r = pl.ds(i * step, step)
        img_k.append(send_img(images.at[r, theirs], img_all.at[own, r], kp))
    for i in range(chunks):
        r = pl.ds(i * step, step)
        send_img(images.at[r, mine], img_all.at[own, r], cp)
    local = [
        pltpu.make_async_copy(own_refs, ref_all.at[slot], lsem.at[0]),
        pltpu.make_async_copy(images.at[:, mine], img_all.at[own], lsem.at[1]),
    ]
    for x in local:
        x.start()

    waited = []

    def forward_img(i):
        r = pl.ds(i * step, step)
        img_k[i].wait_recv()
        waited.append(img_k[i])
        send_img(img_all.at[other, r], img_all.at[other, r], cp)

    def arrive(copy):
        copy.wait_recv()
        waited.append(copy)

    arrive(pair_ref)
    pair_slot = slot + 1 - 2 * k
    for j, (b, w) in enumerate(order):
        stage[j].append((send_ref(ref_all.at[pair_slot], pair_slot, flip(d, b)), pair_slot))
    done_img = 0
    for j, (b, w) in enumerate(order[:-1]):
        bj = bit(d, b)
        for copy, s in stage[j]:
            if done_img < chunks:
                forward_img(done_img)
                done_img += 1
            arrive(copy)
            got = s + w * (1 - 2 * bj)
            for j2 in range(j + 1, len(order)):
                stage[j2].append((send_ref(ref_all.at[got], got, flip(d, order[j2][0])), got))
    while done_img < chunks:
        forward_img(done_img)
        done_img += 1
    for copy in ref_copies + img_copies:
        if all(copy is not x for x in waited):
            copy.wait_recv()
    for copy in ref_copies + img_copies:
        copy.wait_send()
    for x in local:
        x.wait()


def gather(n, images, refs):
    rows, cols = images.shape
    chunks = 4
    n_ref = 1 + sum(2 ** (j + 1) for j in range(len(image_bits(n))))
    n_img = 3 * chunks
    hbm = pl.BlockSpec(memory_space=pl.ANY)
    return pl.pallas_call(
        functools.partial(gather_kernel, n, chunks),
        out_shape=(
            jax.ShapeDtypeStruct((4, rows, cols // 2), images.dtype),
            jax.ShapeDtypeStruct((n // 2, refs.shape[0], cols // 2), refs.dtype),
        ),
        in_specs=[hbm, hbm],
        out_specs=(hbm, hbm),
        scratch_shapes=[
            pltpu.SemaphoreType.DMA((2,)),
            pltpu.SemaphoreType.DMA((n_img,)),
            pltpu.SemaphoreType.DMA((n_img,)),
            pltpu.SemaphoreType.DMA((n_ref,)),
            pltpu.SemaphoreType.DMA((n_ref,)),
        ],
        compiler_params=pltpu.CompilerParams(
            collective_id=0, has_side_effects=True, vmem_limit_bytes=56 * 2**20),
    )(images, refs)


def sums_kernel(n, tiles, post, normed, out, *scratch):
    d = lax.axis_index("img")
    bits = image_bits(n)
    nr = len(bits)
    k, kp = bit(d, PIXEL_BIT), flip(d, PIXEL_BIT)
    q = normed.shape[1]
    w = q // tiles
    partners = [flip(d, b) for b in bits]
    mybits = [bit(d, b) for b in bits]
    keep = scratch[0]
    sends = scratch[1:1 + nr]
    recvs = scratch[1 + nr:1 + 2 * nr]
    last, ssem, rsem = scratch[1 + 2 * nr:]
    half0 = post.shape[1]

    greet([kp] + partners)

    def cols(t):
        return pl.ds(pl.multiple_of(t * w, 128), w)

    def stage_copy(j, t):
        return pltpu.make_async_remote_copy(
            src_ref=sends[j].at[t], dst_ref=recvs[j].at[t],
            send_sem=ssem.at[j, t], recv_sem=rsem.at[j, t],
            device_id={"img": partners[j]}, device_id_type=MESH)

    def last_copy(t):
        place = pl.ds(pl.multiple_of(k * q + t * w, 128), w)
        return pltpu.make_async_remote_copy(
            src_ref=last.at[t], dst_ref=out.at[:, place],
            send_sem=ssem.at[nr, t], recv_sem=rsem.at[nr, t],
            device_id={"img": kp}, device_id_type=MESH)

    def first(t, _):
        sends[0][t] = jnp.dot(
            post[1 - mybits[0]], normed[:, cols(t)], preferred_element_type=jnp.float32
        ).astype(jnp.bfloat16)
        stage_copy(0, t).start()
        return 0

    lax.fori_loop(0, tiles, first, 0)

    def second(t, _):
        keep[t] = jnp.dot(
            post[mybits[0]], normed[:, cols(t)], preferred_element_type=jnp.float32)
        return 0

    lax.fori_loop(0, tiles, second, 0)

    def absorb(j, t):
        stage_copy(j, t).wait_recv()
        size = half0 >> (j + 1)
        there = pl.ds(pl.multiple_of((1 - (mybits[j + 1] if j + 1 < nr else k)) * size, 16), size)
        here = pl.ds(pl.multiple_of((mybits[j + 1] if j + 1 < nr else k) * size, 16), size)
        gone = keep[t, there, :] + recvs[j][t, there, :].astype(jnp.float32)
        if j + 1 < nr:
            sends[j + 1][t] = gone.astype(jnp.bfloat16)
            stage_copy(j + 1, t).start()
        else:
            last[t] = gone
            last_copy(t).start()
        held = keep[t, here, :] + recvs[j][t, here, :].astype(jnp.float32)
        if j + 1 < nr:
            keep[t, 0:size, :] = held
        else:
            out[:, pl.ds(pl.multiple_of(k * q + t * w, 128), w)] = held

    for t in range(tiles + nr - 1):
        for j in range(nr):
            if 0 <= t - j < tiles:
                absorb(j, t - j)

    def finish(t, _):
        last_copy(t).wait()
        for j in range(nr):
            stage_copy(j, t).wait_send()
        return 0

    lax.fori_loop(0, tiles, finish, 0)


def view_sum_blocks(n, post, normed, block_rows):
    bits = image_bits(n)
    nr = len(bits)
    q = normed.shape[1]
    tiles = 8
    w = q // tiles
    half0 = post.shape[1]
    vm = pl.BlockSpec(memory_space=pltpu.VMEM)
    moving = [pltpu.VMEM((tiles, half0 >> j, w), jnp.bfloat16) for j in range(nr)]
    return pl.pallas_call(
        functools.partial(sums_kernel, n, tiles),
        out_shape=jax.ShapeDtypeStruct((block_rows, 2 * q), jnp.float32),
        in_specs=[vm, vm],
        out_specs=vm,
        scratch_shapes=[pltpu.VMEM((tiles, half0, w), jnp.float32)] + moving + moving + [
            pltpu.VMEM((tiles, block_rows, w), jnp.float32),
            pltpu.SemaphoreType.DMA((nr + 1, tiles)),
            pltpu.SemaphoreType.DMA((nr + 1, tiles)),
        ],
        compiler_params=pltpu.CompilerParams(
            collective_id=1, has_side_effects=True, vmem_limit_bytes=56 * 2**20),
    )(post, normed)


def pair_perm(n, value):
    return [(i, i ^ value) for i in range(n)]


def on_device(images, references, cycle_mask, view_class):
    n = lax.axis_size("img")
    m = lax.axis_size("pix")
    d = lax.axis_index("img")
    k, c = bit(d, PIXEL_BIT), bit(d, VIEW_BIT)
    bits = image_bits(n)
    nr = len(bits)
    rows, pixels = images.shape
    q = pixels // 2
    nviews = references.shape[0]
    total_images = rows * n

    widened = images.astype(jnp.float32)
    col_sum, col_sq = lax.psum((jnp.sum(widened, 0), jnp.sum(widened * widened, 0)), "img")
    img_all, ref_all = gather(n, images, references)

    def quarter(x):
        return lax.dynamic_slice_in_dim(x, k * q, q)

    pix_mean = quarter(col_sum) / total_images
    pix_std = jnp.sqrt(quarter(col_sq) / total_images - pix_mean * pix_mean + EPSILON)
    weight = quarter(cycle_mask).astype(jnp.float32)
    img_all = img_all.reshape(4 * rows, q)
    whitened = (img_all.astype(jnp.float32) - pix_mean) / pix_std
    parts = jnp.concatenate([
        jnp.sum(whitened * weight, 1),
        jnp.sum(whitened * whitened * weight, 1),
        jnp.broadcast_to(jnp.sum(weight), (128,)),
    ])
    parts = lax.psum(parts, "pix")
    parts = parts + lax.ppermute(parts, "img", pair_perm(n, PIXEL_BIT))
    count = parts[-1]
    bg_mean = parts[:4 * rows] / count
    bg_std = jnp.sqrt(parts[4 * rows:8 * rows] / count - bg_mean * bg_mean + EPSILON)
    normed = ((whitened - bg_mean[:, None]) / bg_std[:, None]).astype(jnp.bfloat16)

    views = ref_all.reshape(-1, q)
    energy = jnp.sum(jnp.square(views.astype(jnp.float32)), 1)
    raw = lax.dot_general(
        normed, views, (((1,), (1,)), ((), ())), preferred_element_type=jnp.float32)
    partial_value = (raw - 0.5 * energy[None, :]).reshape(4, rows, -1)
    share = lax.psum_scatter(partial_value, "pix", scatter_dimension=1, tiled=True)
    scores = (share + lax.ppermute(share, "img", pair_perm(n, PIXEL_BIT))) * (4.0 / SIDE)

    row_max = jnp.max(scores, 2)
    row_exp = jnp.sum(jnp.exp(scores - row_max[..., None]), 2)
    row_sum = jnp.sum(scores, 2)
    here = jnp.stack([row_max, row_exp, row_sum])
    there = lax.ppermute(here, "img", pair_perm(n, VIEW_BIT))
    both_max = jnp.maximum(here[0], there[0])
    both_exp = here[1] * jnp.exp(here[0] - both_max) + there[1] * jnp.exp(there[0] - both_max)
    log_total = both_max + jnp.log(both_exp)
    nref = nviews * n
    evidence = log_total - (here[2] + there[2]) / nref
    evidence = lax.dynamic_index_in_dim(evidence, 2 * c + k, 0, keepdims=False)
    posterior = jnp.exp(scores - log_total[..., None]).astype(jnp.bfloat16)
    posterior = lax.all_gather(posterior, "pix", axis=1, tiled=True)
    posterior = posterior.reshape(4 * rows, -1)

    normed = lax.optimization_barrier(normed)
    view_sums = view_sum_blocks(n, posterior.T.reshape(2, -1, 4 * rows), normed, nviews)

    class_mass = jnp.sum(posterior, 0, dtype=jnp.float32).reshape(n // 2, nviews)
    slots = jnp.arange(n // 2)
    owner = (slots % 2) * PIXEL_BIT + c * VIEW_BIT
    for j, b in enumerate(bits):
        owner = owner + ((slots // 2 ** (nr - j)) % 2) * b
    classes = view_class.reshape(n, nviews)[owner]
    onehot = (classes.reshape(-1)[:, None] == jnp.arange(NCLS, dtype=jnp.int32)[None, :]).astype(jnp.float32)
    class_local = jnp.dot(class_mass.reshape(-1), onehot, precision=lax.Precision.HIGHEST)
    class_total = 0.5 * lax.psum(class_local, "img")
    return (view_sums, class_total * (NCLS / total_images), evidence.reshape(-1))


def solution(mesh):
    in_specs = (P("img", "pix"), P("img", "pix"), P("pix"), P())
    out_specs = (P("img", "pix"), P(), P(("img", "pix")))
    return jax.shard_map(
        on_device, mesh=mesh, in_specs=in_specs, out_specs=out_specs, check_vma=False
    )
```

time: 1170 us -> 399 us (0.34)
  waiting for transfers between devices: 1050 us -> 70.2 us
  Pallas kernels: 0 us -> 212 us
  matrix products: 36.9 us -> 8.67 us
  other arithmetic: 24.9 us -> 37 us
    reduce_scatter x1, waiting for transfers between devices: 654 us -> 9.89 us  [on_device(): lax.psum_scatter(partial_value, 'pix', scatter_dimension=1, tiled=True)]
    all_gather x1, waiting for transfers between devices: 265 us -> 1.41 us  [on_device(): posterior = lax.all_gather(posterior, 'pix', axis=1, tiled=True)]
    pallas_call x0 -> x2, Pallas kernels: none -> 212 us  [the longest x1 118 us: gather(): pl.pallas_call(functools.partial(gather_kernel, n, chunks), out_shape=(ja...]
    psum x1, waiting for transfers between devices: 107 us -> 19.7 us  [on_device(): lax.psum((jnp.sum(widened, 0), jnp.sum(widened * widened, 0)), 'img')]
    ppermute x0 -> x3, waiting for transfers between devices: none -> 39.1 us  [the longest x1 35.1 us: on_device(): lax.ppermute(share, 'img', pair_perm(n, PIXEL_BIT))]
    dot_general x3 -> x2, matrix products: 36.9 us -> 8.67 us  [the longest x1 8.34 us: on_device(): lax.dot_general(normed, views, (((1,), (1,)), ((), ())), preferred_elemen...]
    psum x1 -> x0, waiting for transfers between devices: 18.5 us -> none  [on_device(): scores = lax.psum(partial_value, 'pix') * factor]
    convert_element_type x1 -> x3, other arithmetic: 0.01 us -> 16.8 us  [the longest x2 15.7 us: on_device(): ((whitened - bg_mean[:, None]) / bg_std[:, None]).astype(jnp.bfloat16)]
  transfers between devices with their start and end apart: 4 -> 6, of which waited for: 4 -> 6; matrix products, arithmetic and copies ran while one was open for 1% -> 4% of each run, Pallas kernels for 0% -> 30%
where the time goes in v1:
time: 399 us; the launch traced here: 398 us
  Pallas kernels  212 us (53%)
  waiting for transfers between devices  70.2 us (18%)
  blocking collectives  43.1 us (11%)
  other arithmetic  37 us (9%)
  between operations  14 us (4%)
  local copies, waits for them, and re-layouts  9.02 us (2%)
  matrix products  8.67 us (2%)
  starting transfers between devices  4.58 us (1%)
    pallas_call x1, Pallas kernels, gather(): pl.pallas_call(functools.partial(gather_kernel, n, chunks), out_shape=(ja...  118 us
    pallas_call x1, Pallas kernels, view_sum_blocks(): pl.pallas_call(functools.partial(sums_kernel, n, tiles), out_shape=jax.Sh...  93.7 us
    psum x1, blocking collectives, on_device(): class_total = 0.5 * lax.psum(class_local, 'img')  39.8 us
    ppermute x1, waiting for transfers between devices, on_device(): lax.ppermute(share, 'img', pair_perm(n, PIXEL_BIT))  35.1 us
    psum x1, waiting for transfers between devices, on_device(): lax.psum((jnp.sum(widened, 0), jnp.sum(widened * widened, 0)), 'img')  19.7 us
    convert_element_type x2, other arithmetic, on_device(): ((whitened - bg_mean[:, None]) / bg_std[:, None]).astype(jnp.bfloat16)  15.7 us
    reduce_scatter x1, waiting for transfers between devices, on_device(): lax.psum_scatter(partial_value, 'pix', scatter_dimension=1, tiled=True)  9.89 us
    dot_general x1, matrix products, on_device(): lax.dot_general(normed, views, (((1,), (1,)), ((), ())), preferred_elemen...  8.34 us
  transfers between devices with their start and end apart: 6, of which 6 were waited for; matrix products, arithmetic and copies ran while one was open for 4% of the time, Pallas kernels for 30%

profile of v1, /device:TPU:0, one launch (start us, length us, event | category | flops | bytes accessed | tf_op | source)
XLA Modules:
  0.0 398.2 jit_solution(5099234161662360730)
XLA Ops:
  7.2 0.0 copy-start.1
  7.2 0.0 all-reduce.3.cloned.1.call-start
  7.2 4.0 %convert_reduce_fusion = (f32[8192]{0:T(1024)}, f32[8192]{0:T(1024)}) fusion(bf16[256,8192]{1,0:T(8,128)(2,1)} %images.1), kind=kLoop, calls=%fused_computation.12 | loop fusion | flops 8372224 | bytes 4259840 | tf_op jit(solution)/shard_map/reduce_sum | solution.py:286
  11.2 0.0 all-reduce.3.cloned.1.call-update
  11.2 0.0 reduce-scatter.2.cloned.1.call-start
  11.3 118.0 %shard_map.67 = (bf16[4,256,4096]{2,1,0:T(8,128)(2,1)}, bf16[8,96,4096]{2,1,0:T(8,128)(2,1)}) custom-call(bf16[256,8192]{1,0:T(8,128)(2,1)} %images.1, bf16[96,8192]{1,0:T(8,128)(2,1)} %refs.1), custom_call_target="tpu_custom_call" | custom-call | tf_op jit(solution)/shard_map/pallas_call | solution.py:144
  129.4 4.1 %multiply_reduce_fusion.2 = f32[8,96]{1,0:T(8,128)S(1)} fusion(bf16[8,96,4096]{2,1,0:T(8,128)(2,1)} %get-tuple-element.6), kind=kLoop, calls=%fused_computation.10 | loop fusion | flops 9436416 | bytes 6294528 | tf_op jit(solution)/shard_map/reduce_sum | solution.py:310
  133.5 0.0 copy-done.1
  133.5 0.6 fusion.25
  134.1 19.7 %all-reduce.3.cloned.1.call-done = (f32[8192]{0:T(1024)}, f32[8192]{0:T(1024)}) async-done(((f32[8192]{0:T(1024)}, f32[8192]{0:T(1024)}), (f32[8192]{0:T(1024)}, f32[8192]{0:T(1024)})) %all-reduce.3.cloned.1.call-update) | async-done | bytes 65552 | tf_op jit(solution)/shard_map/psum | solution.py:286
  153.8 0.7 dynamic-slice_multiply_fusion
  154.6 0.0 slice-start
  154.6 7.1 %multiply_reduce_fusion.1 = (f32[4,256]{1,0:T(4,128)S(1)}, f32[4,256]{1,0:T(4,128)S(1)}) fusion(f32[4096]{0:T(1024)S(1)} %get-tuple-element.23, f32[4096]{0:T(1024)S(1)} %get-tuple-element.25, f32[4096]{0:T(1024)S(1)} %get-tuple-element.24, bf16[4,256,4096]{2,1,0:T(8,128)(2,1)} %get-tuple-element.5), kind=kLoop, calls=%fused_computation.7 | loop fusion | flops 33552384 | bytes 8445952 | tf_op jit(solution)/shard_map/reduce_sum | solution.py:298
  161.7 0.6 broadcast_in_dim.2
  162.4 3.3 psum.30
  165.7 0.8 collective-permute-start
  166.4 0.1 mul.113
  166.5 2.8 collective-permute-done
  169.4 0.6 slice.28
  169.9 0.7 add_sqrt_fusion.1
  170.6 0.0 slice-start.1
  170.6 6.5 %divide_convert_fusion = bf16[4,256,4096]{2,1,0:T(8,128)(2,1)S(1)} fusion(f32[4,256]{1,0:T(4,128)S(1)} %add_sqrt_fusion.2, f32[4,256]{1,0:T(4,128)S(1)} %div.93, f32[4096]{0:T(1024)S(1)} %get-tuple-element.25, f32[4096]{0:T(1024)S(1)} %get-tuple-element.24, bf16[4,256,4096]{2,1,0:T(8,128)(2,1)} %get-tuple-element.5), kind=kLoop, calls=%fused_computation.5 | loop fusion | flops 25165824 | bytes 16818176 | tf_op jit(solution)/shard_map/convert_element_type | solution.py:307
  177.1 0.0 slice-done
  177.1 0.0 slice-done.1
  177.1 8.3 %convolution_subtract_fusion = f32[1024,768]{1,0:T(8,128)} fusion(bf16[1024,4096]{1,0:T(8,128)(2,1)S(1)} %bitcast.58, bf16[768,4096]{1,0:T(8,128)(2,1)S(1)} %bitcast.63, f32[768]{0:T(1024)S(1)} %mul.113), kind=kOutput, calls=%fused_computation.15 | convolution fusion | flops 6443237376 | bytes 17828864 | tf_op jit(solution)/shard_map/dot_general | solution.py:311
  185.5 0.0 copy-start.2
  185.5 0.0 reduce-scatter.2.cloned.1.call-update
  185.5 0.2 all-gather.2.cloned.1.call-start
  185.7 9.9 %reduce-scatter.2.cloned.1.call-done = f32[4,128,768]{2,1,0:T(8,128)} async-done(((f32[4,256,768]{2,1,0:T(8,128)}), f32[4,128,768]{2,1,0:T(8,128)}) %reduce-scatter.2.cloned.1.call-update) | async-done | bytes 1572880 | tf_op jit(solution)/shard_map/reduce_scatter | solution.py:314
  195.6 1.7 collective-permute-start.1
  197.4 35.1 %collective-permute-done.1 = f32[4,128,768]{2,1,0:T(8,128)S(1)} collective-permute-done((f32[4,128,768]{2,1,0:T(8,128)}, f32[4,128,768]{2,1,0:T(8,128)S(1)}, u32[]{:S(2)}, u32[]{:S(2)}) %collective-permute-start.1) | collective-permute-done | bytes 1572896 | tf_op jit(solution)/shard_map/ppermute | solution.py:315
  232.4 1.6 fusion.24
  234.1 0.4 exponential_reduce_fusion
  234.5 1.8 collective-permute-start.2
  236.3 0.0 copy-done.2
  236.3 0.1 reshape.288
  236.4 0.6 gather_fusion
  237.0 0.1 eq.22
  237.0 1.2 collective-permute-done.2
  238.2 1.2 exponential_convert_fusion
  239.4 0.0 all-gather.2.cloned.1.call-update
  239.4 9.2 %fusion.3.normed = bf16[1024,4096]{1,0:T(8,128)(2,1)} fusion(f32[1024]{0:T(1024)S(1)} %get-tuple-element.17, f32[1024]{0:T(1024)S(1)} %get-tuple-element.18, f32[4096]{0:T(1024)S(1)} %get-tuple-element.25, f32[4096]{0:T(1024)S(1)} %get-tuple-element.24, bf16[4,256,4096]{2,1,0:T(8,128)(2,1)} %get-tuple-element.5), kind=kLoop, calls=%fused_computation.9 | loop fusion | flops 25165824 | bytes 16818176 | tf_op jit(solution)/shard_map/convert_element_type | solution.py:307
  248.6 0.5 dynamic-slice_bitcast_fusion
  249.2 1.4 all-gather.2.cloned.1.call-done
  250.6 0.0 copy-start
  250.6 2.7 copy.8
  253.3 93.7 %shard_map.68 = f32[96,8192]{1,0:T(8,128)} custom-call(bf16[2,384,1024]{2,1,0:T(8,128)(2,1)} %bitcast.60, bf16[1024,4096]{1,0:T(8,128)(2,1)} %fusion.3.normed), custom_call_target="tpu_custom_call" | custom-call | tf_op jit(solution)/shard_map/pallas_call | solution.py:254
  347.0 0.0 copy-done
  347.0 0.3 convert_reduce_fusion.1
  347.3 0.3 convolution_bitcast_fusion
  347.6 39.8 %psum.31 = f32[96]{0:T(128)S(1)} all-reduce(f32[96]{0:T(128)S(1)} %convolution_bitcast_fusion), channel_id=1, replica_groups=mesh['img'=16,'pix'=2] {'img'}, use_global_device_ids=true, to_apply=%region_14.15 | all-reduce | flops 96 | bytes 768 | tf_op jit(solution)/shard_map/psum | solution.py:343
  387.4 0.5 broadcast_multiply_fusion.1
  387.9 3.8 copy.14
  (14 shorter events, 0.1 us)
Async XLA Ops:
  7.2 126.3 %copy-start.1 = (s32[8192]{0:T(1024)S(1)}, s32[8192]{0:T(1024)}, u32[]{:S(2)}) copy-start(s32[8192]{0:T(1024)} %param.6) | copy-start | bytes 98308
  7.2 146.6 %all-reduce.3.cloned.1.call-start = ((), (), s32[]{:S(2)}) async-start(), calls=%async_computation.3 | async-start | bytes 131072 | tf_op jit(solution)/shard_map/psum | solution.py:286
  11.2 184.4 %reduce-scatter.2.cloned.1.call-start = ((), (), s32[]{:S(2)}) async-start(), calls=%async_computation.1 | async-start | bytes 4718592 | tf_op jit(solution)/shard_map/reduce_scatter | solution.py:314
  154.6 22.5 %slice-start = ((s8[6291456]{0:T(1024)(128)(4,1)}), s8[2097152]{0:T(1024)(128)(4,1)S(1)}, s32[]{:S(2)}) async-start(s8[6291456]{0:T(1024)(128)(4,1)} %bitcast.61), calls=%async_computation.4 | async-start | bytes 4194304
  165.7 3.7 collective-permute-start
  170.6 6.5 %slice-start.1 = ((s8[6291456]{0:T(1024)(128)(4,1)}), s8[4194304]{0:T(1024)(128)(4,1)S(1)}, s32[]{:S(2)}) async-start(s8[6291456]{0:T(1024)(128)(4,1)} %bitcast.61), calls=%async_computation.5 | async-start | bytes 8388608
  185.5 50.8 %copy-start.2 = (s32[1536]{0:T(1024)S(1)}, s32[1536]{0:T(1024)}, u32[]{:S(2)}) copy-start(s32[1536]{0:T(1024)} %param.7) | copy-start | bytes 18436
  185.5 65.1 %all-gather.2.cloned.1.call-start = ((), (), s32[]{:S(2)}) async-start(), calls=%async_computation.2 | async-start | bytes 2359296 | tf_op jit(solution)/shard_map/all_gather | solution.py:329
  195.6 36.8 %collective-permute-start.1 = (f32[4,128,768]{2,1,0:T(8,128)}, f32[4,128,768]{2,1,0:T(8,128)S(1)}, u32[]{:S(2)}, u32[]{:S(2)}) collective-permute-start(f32[4,128,768]{2,1,0:T(8,128)} %reduce-scatter.2.cloned.1.call-done), channel_id=1, source_target_pairs={{0,8},{2,10},{4,12},{6,14},{8,0},{10,2},{12,4},{14,6},{16,24},{18,... | collective-permute-start | bytes 4718600 | tf_op jit(solution)/shard_map/ppermute | solution.py:315
  234.5 3.7 collective-permute-start.2
  250.6 96.4 %copy-start = (bf16[4,256,768]{2,1,0:T(8,128)(2,1)S(1)}, bf16[4,256,768]{2,1,0:T(8,128)(2,1)}, u32[]{:S(2)}) copy-start(bf16[4,256,768]{2,1,0:T(8,128)(2,1)} %all-gather.2.cloned.1.call-done) | copy-start | bytes 4718596
Sparse Core Ops, SparseCore 0:
  14.2 139.6 all-reduce.2
  185.6 9.9 reduce-scatter.1
  239.6 10.9 all-gather.1

commit v2 on v0

v2 whole, which is shorter than its diff:
```python
import functools

import jax
import jax.numpy as jnp
from jax import lax
from jax.experimental import pallas as pl
from jax.experimental.pallas import tpu as pltpu
from jax.sharding import PartitionSpec as P

SIDE = 128
NCLS = 96
EPSILON = 1e-05
MESH = pl.DeviceIdType.MESH
F32 = jnp.float32
BF16 = jnp.bfloat16

PIXEL_BIT = 4
VIEW_BIT = 2
CHUNKS = 4
TILES = 8


def image_bits(n):
    return [b for b in (1, *reversed([2**j for j in range(3, 20) if 2**j < n]))]


def low_bits(m):
    return [2**j for j in range(20) if 2**j < m]


def bit(index, value):
    return (index // value) % 2


def flip(index, value):
    return index + value * (1 - 2 * bit(index, value))


def aligned(start, size, unit):
    return pl.ds(pl.multiple_of(start, unit), size)


def kernel(n, m, images, refs, mask, classes, out, ev_out, cls_out,
           img_all, pair_img, ref_all, stat, stat_in, col, bg, bg_mine, bg_in,
           ecol, erow, partial, halves, soft, soft_in, evb, post, post_t,
           mass, mass_in, fresh, keep, sends, recvs, last,
           lsem, isend, irecv, rsend, rrecv, tsend, trecv, bsend, brecv,
           hsend, hrecv, csend, crecv, gsend, grecv, vsend, vrecv, ksend, krecv,
           esend, erecv):
    d = lax.axis_index("img")
    p = lax.axis_index("pix")
    bits = image_bits(n)
    nr = len(bits)
    pbits = list(reversed(low_bits(m)))
    k, c = bit(d, PIXEL_BIT), bit(d, VIEW_BIT)
    kp, cp = flip(d, PIXEL_BIT), flip(d, VIEW_BIT)
    rows, cols = images.shape
    nviews = refs.shape[0]
    q = cols // 2
    mine = aligned(k * q, q, 128)
    theirs = aligned((1 - k) * q, q, 128)
    weights = [2 ** (nr - j) for j in range(nr)]
    slot = k
    for b, w in zip(bits, weights):
        slot = slot + w * bit(d, b)
    own = 2 * c + k
    other = 2 * c + 1 - k
    across = 2 * (1 - c) + k
    diag = 2 * (1 - c) + 1 - k

    barrier = pltpu.get_barrier_semaphore()
    img_partners = [kp, cp] + [flip(d, b) for b in bits]
    for x in img_partners:
        pl.semaphore_signal(barrier, inc=1, device_id={"img": x}, device_id_type=MESH)
    for b in pbits:
        pl.semaphore_signal(barrier, inc=1, device_id={"pix": flip(p, b)}, device_id_type=MESH)
    pl.semaphore_wait(barrier, len(img_partners) + len(pbits))

    def remote(src, dst, ssem, rsem, axis, partner):
        return pltpu.make_async_remote_copy(
            src_ref=src, dst_ref=dst, send_sem=ssem, recv_sem=rsem,
            device_id={axis: partner}, device_id_type=MESH)

    ref_copies = []
    img_copies = []
    waited = []

    def send_ref(src, s, partner):
        i = len(ref_copies)
        x = remote(src, ref_all.at[s], rsend.at[i], rrecv.at[i], "img", partner)
        x.start()
        ref_copies.append(x)
        return x

    def send_img(src, dst, partner):
        i = len(img_copies)
        x = remote(src, dst, isend.at[i], irecv.at[i], "img", partner)
        x.start()
        img_copies.append(x)
        return x

    def arrive(x):
        if all(x is not y for y in waited):
            x.wait_recv()
            waited.append(x)

    step = rows // CHUNKS

    def chunk(i):
        return pl.ds(i * step, step)

    order = list(reversed(list(zip(bits, weights))))
    pair_ref = send_ref(refs.at[:, theirs], slot, kp)
    stage = [[] for _ in order]
    for j, (b, w) in enumerate(order):
        stage[j].append((send_ref(refs.at[:, mine], slot, flip(d, b)), slot))
    img_across = send_img(images.at[:, mine], img_all.at[own], cp)
    own_ref = pltpu.make_async_copy(refs.at[:, mine], ref_all.at[slot], lsem.at[0])
    own_ref.start()

    wide = min(512, cols)

    def col_tile(t, _):
        at = aligned(t * wide, wide, 128)
        x = images[:, at].astype(F32)
        stat[0, 0:1, at] = jnp.sum(x, 0, keepdims=True)
        stat[0, 1:2, at] = jnp.sum(x * x, 0, keepdims=True)
        return 0

    lax.fori_loop(0, cols // wide, col_tile, 0)
    img_k = []
    hops = [*bits, VIEW_BIT, PIXEL_BIT]
    for j, b in enumerate(hops):
        x = remote(stat.at[j], stat_in.at[j], tsend.at[j], trecv.at[j], "img", flip(d, b))
        x.start()
        x.wait()
        stat[j + 1] = stat[j] + stat_in[j]
        if j == 1:
            img_k.append(send_img(images.at[chunk(0), theirs], pair_img.at[chunk(0)], kp))
    total = rows * n
    nh = len(hops)
    col_mean = stat[nh, 0:1, :] / total
    col[0:1, :] = col_mean
    col[1:2, :] = 1.0 / jnp.sqrt(stat[nh, 1:2, :] / total - col_mean * col_mean + EPSILON)

    arrive(pair_ref)
    pair_slot = slot + 1 - 2 * k
    for j, (b, w) in enumerate(order):
        stage[j].append((send_ref(ref_all.at[pair_slot], pair_slot, flip(d, b)), pair_slot))
    img_k.append(send_img(images.at[chunk(1), theirs], pair_img.at[chunk(1)], kp))

    def bg_tile(t, carry):
        s, sq, cnt = carry
        at = aligned(t * wide, wide, 128)
        w = (images[:, at].astype(F32) - col[0:1, at]) * col[1:2, at]
        mk = mask[:, at].astype(F32)
        wm = w * mk
        wq = wm * w
        for i in range(wide // 128):
            part = slice(i * 128, (i + 1) * 128)
            s = s + wm[:, part]
            sq = sq + wq[:, part]
            cnt = cnt + mk[:, part]
        return s, sq, cnt

    zero = jnp.zeros((rows, 128), F32)
    s, sq, cnt = lax.fori_loop(0, cols // wide, bg_tile, (zero, zero, jnp.zeros((1, 128), F32)))
    lane = lax.broadcasted_iota(jnp.int32, (rows, 128), 1)
    bg_mine[0] = jnp.where(
        lane == 0, jnp.sum(s, 1, keepdims=True),
        jnp.where(lane == 1, jnp.sum(sq, 1, keepdims=True), jnp.sum(cnt, 1, keepdims=True)))
    for j, b in enumerate(pbits):
        x = remote(bg_mine.at[j], bg_in.at[j], bsend.at[j], brecv.at[j], "pix", flip(p, b))
        x.start()
        x.wait()
        bg_mine[j + 1] = bg_mine[j] + bg_in[j]
    np_ = len(pbits)
    sums = bg_mine[np_]
    count = sums[:, 2:3]
    bg_mean = sums[:, 0:1] / count
    bg_inv = 1.0 / jnp.sqrt(sums[:, 1:2] / count - bg_mean * bg_mean + EPSILON)
    bg[own] = jnp.where(lane == 0, bg_mean, bg_inv)
    bg_k = remote(bg.at[own], bg.at[own], bsend.at[np_], brecv.at[np_], "img", kp)
    bg_k.start()
    bg_c = remote(bg.at[own], bg.at[own], bsend.at[np_ + 1], brecv.at[np_ + 1], "img", cp)
    bg_c.start()

    ncol = min(512, q)

    def normalise(read, s):
        def tile(t, _):
            at = aligned(t * ncol, ncol, 128)
            there = aligned(k * q + t * ncol, ncol, 128)
            w = (read(t, at, there).astype(F32) - col[0:1, there]) * col[1:2, there]
            img_all[s, :, at] = ((w - bg[s, :, 0:1]) * bg[s, :, 1:2]).astype(BF16)
            return 0
        lax.fori_loop(0, q // ncol, tile, 0)

    normalise(lambda t, at, there: images[:, there], own)

    def energy(s):
        def tile(t, acc):
            x = ref_all[s, :, aligned(t * ncol, ncol, 128)].astype(F32)
            x = x * x
            for i in range(ncol // 128):
                acc = acc + x[:, i * 128:(i + 1) * 128]
            return acc
        acc = lax.fori_loop(0, q // ncol, tile, jnp.zeros((nviews, 128), F32))
        ecol[s] = jnp.broadcast_to(jnp.sum(acc, 1, keepdims=True), (nviews, 128))

    bg_k.wait_recv()
    bg_d = remote(bg.at[other], bg.at[other], bsend.at[np_ + 2], brecv.at[np_ + 2], "img", cp)
    bg_d.start()

    sent_k = [2]

    def next_k():
        i = sent_k[0]
        if i < CHUNKS:
            img_k.append(send_img(images.at[chunk(i), theirs], pair_img.at[chunk(i)], kp))
            sent_k[0] += 1

    fwd = []

    def forward_img():
        i = len(fwd)
        if i < CHUNKS:
            arrive(img_k[i])
            fwd.append(send_img(pair_img.at[chunk(i)], img_all.at[other, chunk(i)], cp))
            next_k()

    for j, (b, w) in enumerate(order[:-1]):
        for x, s in stage[j]:
            arrive(x)
            got = s + w * (1 - 2 * bit(d, b))
            for j2 in range(j + 1, len(order)):
                stage[j2].append((send_ref(ref_all.at[got], got, flip(d, order[j2][0])), got))
            forward_img()
    while len(fwd) < CHUNKS:
        forward_img()
    normalise(lambda t, at, there: pair_img[:, at], other)
    own_ref.wait()
    energy(slot)
    energy(pair_slot)
    for j, (b, w) in enumerate(order):
        for x, s in stage[j]:
            arrive(x)
            energy(s + w * (1 - 2 * bit(d, b)))
    erow[...] = jnp.transpose(ecol[...].reshape(-1, 128))[0:8]

    nv = nviews * n // 2
    kt = min(1024, q)

    def score(s):
        partial[s] = jnp.broadcast_to(-0.5 * erow[0:1, :], (rows, nv))

        def tile(t, _):
            at = aligned(t * kt, kt, 128)
            partial[s] += lax.dot_general(
                img_all[s, :, at], ref_all[:, :, at].reshape(nv, kt),
                (((1,), (1,)), ((), ())), preferred_element_type=F32)
            return 0
        lax.fori_loop(0, q // kt, tile, 0)

    cuts = [("pix", b, flip(p, b), bit(p, b)) for b in pbits] + [("img", PIXEL_BIT, kp, k)]
    nc = len(cuts)
    starts, sizes = [0], [rows]
    for axis, b, partner, mybit in cuts:
        sizes.append(sizes[-1] // 2)
        starts.append(starts[-1] + mybit * sizes[-1])

    def halve(j, s):
        axis, b, partner, mybit = cuts[j]
        gone = aligned(starts[j] + (1 - mybit) * sizes[j + 1], sizes[j + 1], sizes[j + 1])
        return remote(partial.at[s, gone], halves[j].at[s], hsend.at[j, s], hrecv.at[j, s], axis, partner)

    def absorb_half(j, s):
        halve(j, s).wait_recv()
        held = aligned(starts[j + 1], sizes[j + 1], sizes[j + 1])
        partial[s, held, :] += halves[j][s]

    def slot_of(i):
        return 2 * ((c + i // 2) % 2) + i % 2

    def begin(i, _):
        s = slot_of(i)
        score(s)
        halve(0, s).start()
        return 0

    def middle(j):
        def body(i, _):
            s = slot_of(i)
            absorb_half(j, s)
            halve(j + 1, s).start()
            return 0
        return body

    nlast = sizes[-1]
    held = aligned(starts[-1], nlast, nlast)
    lane2 = lax.broadcasted_iota(jnp.int32, (nlast, 128), 1)

    def soft_copy(s):
        return remote(soft.at[s], soft_in.at[s], csend.at[s], crecv.at[s], "img", cp)

    def soften(i, _):
        s = slot_of(i)
        absorb_half(nc - 1, s)
        x = partial[s, held, :] * (4.0 / SIDE)
        partial[s, held, :] = x
        top = jnp.max(x, 1, keepdims=True)
        soft[s] = jnp.where(
            lane2 == 0, top,
            jnp.where(lane2 == 1, jnp.sum(jnp.exp(x - top), 1, keepdims=True),
                      jnp.sum(x, 1, keepdims=True)))
        soft_copy(s).start()
        return 0

    def grow(j, s):
        axis, b, partner, mybit = cuts[j]
        at = aligned(starts[j + 1], sizes[j + 1], sizes[j + 1])
        return remote(post.at[s, at], post.at[s, at], gsend.at[j, s], grecv.at[j, s], axis, partner)

    def settle(i, _):
        s = slot_of(i)
        soft_copy(s).wait_recv()
        a, b = soft[s], soft_in[s]
        top = jnp.maximum(a[:, 0:1], b[:, 0:1])
        exps = a[:, 1:2] * jnp.exp(a[:, 0:1] - top) + b[:, 1:2] * jnp.exp(b[:, 0:1] - top)
        log_total = top + jnp.log(exps)
        evb[s] = jnp.broadcast_to(
            log_total - (a[:, 2:3] + b[:, 2:3]) / (nviews * n), (nlast, 128))
        post[s, held, :] = jnp.exp(partial[s, held, :] - log_total).astype(BF16)
        grow(nc - 1, s).start()
        return 0

    lax.fori_loop(0, 2, begin, 0)
    for j in range(nc - 1):
        lax.fori_loop(0, 2, middle(j), 0)
    bg_c.wait_recv()
    arrive(img_across)
    normalise(lambda t, at, there: img_all[across, :, at], across)
    bg_d.wait_recv()
    for x in fwd:
        arrive(x)
    normalise(lambda t, at, there: img_all[diag, :, at], diag)
    lax.fori_loop(2, 4, begin, 0)
    lax.fori_loop(0, 2, soften, 0)
    for j in range(nc - 1):
        lax.fori_loop(2, 4, middle(j), 0)
    lax.fori_loop(2, 4, soften, 0)
    lax.fori_loop(0, 4, settle, 0)
    for j in range(nc - 1, 0, -1):
        def grown(i, _, j=j):
            s = slot_of(i)
            grow(j, s).wait_recv()
            grow(j - 1, s).start()
            return 0
        lax.fori_loop(0, 4, grown, 0)

    half0 = nv // 2

    def turn(i, acc):
        s = slot_of(i)
        grow(0, s).wait_recv()
        x = post[s].astype(F32)
        xt = jnp.transpose(x).astype(BF16)
        at = aligned(s * rows, rows, 128)
        post_t[0, :, at] = xt[:half0]
        post_t[1, :, at] = xt[half0:]
        return acc + jnp.sum(x, 0, keepdims=True)

    class_mass = lax.fori_loop(0, 4, turn, jnp.zeros((1, nv), F32))

    wt = q // TILES
    partners = [flip(d, b) for b in bits]
    mybits = [bit(d, b) for b in bits] + [k]

    def tile_cols(t):
        return aligned(t * wt, wt, 128)

    def weigh(half, t):
        return jnp.dot(post_t[half], img_all[:, :, tile_cols(t)].reshape(4 * rows, wt),
                       preferred_element_type=F32)

    def stage_copy(j, t):
        return remote(sends[j].at[t], recvs[j].at[t], vsend.at[j, t], vrecv.at[j, t],
                      "img", partners[j])

    def last_copy(t):
        place = aligned(k * q + t * wt, wt, 128)
        return remote(last.at[t], out.at[:, place], vsend.at[nr, t], vrecv.at[nr, t], "img", kp)

    def first(t, _):
        sends[0][t] = weigh(1 - mybits[0], t).astype(BF16)
        stage_copy(0, t).start()
        return 0

    lax.fori_loop(0, TILES, first, 0)

    ev_out[aligned(k * nlast, nlast, nlast), :] = evb[own]
    ev_copy = remote(evb.at[other], ev_out.at[aligned(k * nlast, nlast, nlast)],
                     esend.at[0], erecv.at[0], "img", kp)
    ev_copy.start()

    hit = lax.broadcasted_iota(jnp.int32, (NCLS, nv), 0) == classes[...]
    mass[0] = jnp.broadcast_to(
        jnp.sum(jnp.where(hit, class_mass, 0.0), 1, keepdims=True), (NCLS, 128))
    mass_hops = [*bits, VIEW_BIT]

    def mass_copy(j):
        return remote(mass.at[j], mass_in.at[j], ksend.at[j], krecv.at[j], "img", flip(d, mass_hops[j]))

    mass_copy(0).start()

    def mass_hop(j):
        if j < len(mass_hops):
            mass_copy(j).wait()
            mass[j + 1] = mass[j] + mass_in[j]
            if j + 1 < len(mass_hops):
                mass_copy(j + 1).start()

    def absorb(j, t):
        size = half0 >> (j + 1)
        there = aligned((1 - mybits[j + 1]) * size, size, 16)
        here = aligned(mybits[j + 1] * size, size, 16)
        if j == 0:
            fresh[...] = weigh(mybits[0], t)
            base = fresh
        else:
            base = keep[j - 1].at[t]
        stage_copy(j, t).wait_recv()
        gone = base[there, :] + recvs[j][t, there, :].astype(F32)
        if j + 1 < nr:
            sends[j + 1][t] = gone.astype(BF16)
            stage_copy(j + 1, t).start()
        else:
            last[t] = gone
            last_copy(t).start()
        rest = base[here, :] + recvs[j][t, here, :].astype(F32)
        if j + 1 < nr:
            keep[j][t] = rest
        else:
            out[:, aligned(k * q + t * wt, wt, 128)] = rest

    def steps(t):
        for j in range(nr):
            absorb(j, t - j)

    def ramp(ts):
        for t in ts:
            for j in range(nr):
                if 0 <= t - j < TILES:
                    absorb(j, t - j)

    ramp(range(nr - 1))
    mass_hop(0)
    lax.fori_loop(nr - 1, TILES // 2, lambda t, _: (steps(t), 0)[1], 0)
    mass_hop(1)
    lax.fori_loop(TILES // 2, TILES, lambda t, _: (steps(t), 0)[1], 0)
    for j in range(2, len(mass_hops)):
        mass_hop(j)
    cls_out[...] = mass[len(mass_hops)] * (NCLS / total)
    ramp(range(TILES, TILES + nr - 1))

    for x in ref_copies + img_copies + [bg_k, bg_c, bg_d]:
        x.wait_send()
    ev_copy.wait()

    def drain(s, _):
        soft_copy(s).wait_send()
        for j in range(nc):
            halve(j, s).wait_send()
            grow(j, s).wait_send()
        return 0

    lax.fori_loop(0, 4, drain, 0)

    def finish(t, _):
        last_copy(t).wait()
        for j in range(nr):
            stage_copy(j, t).wait_send()
        return 0

    lax.fori_loop(0, TILES, finish, 0)


def whole_step(n, m, images, refs, mask, classes):
    rows, cols = images.shape
    nviews = refs.shape[0]
    q = cols // 2
    bits = image_bits(n)
    nr = len(bits)
    nb = nr + 2
    npix = len(low_bits(m))
    nc = npix + 1
    nv = nviews * n // 2
    half0 = nv // 2
    wt = q // TILES
    nlast = rows >> nc
    n_ref = 1 + sum(2 ** (j + 1) for j in range(nr))
    n_img = 1 + 2 * CHUNKS
    vm = pl.BlockSpec(memory_space=pltpu.VMEM)
    hbm = pl.BlockSpec(memory_space=pl.ANY)
    V = pltpu.VMEM
    dma = pltpu.SemaphoreType.DMA
    scratch = [
        V((4, rows, q), BF16), V((rows, q), BF16), V((n // 2, nviews, q), BF16),
        V((nb + 1, 2, cols), F32), V((nb, 2, cols), F32), V((2, cols), F32),
        V((4, rows, 128), F32), V((npix + 1, rows, 128), F32), V((npix, rows, 128), F32),
        V((n // 2, nviews, 128), F32), V((8, nv), F32),
        V((4, rows, nv), F32), [V((4, rows >> (j + 1), nv), F32) for j in range(nc)],
        V((4, nlast, 128), F32), V((4, nlast, 128), F32), V((4, nlast, 128), F32),
        V((4, rows, nv), BF16), V((2, half0, 4 * rows), BF16),
        V((nb, NCLS, 128), F32), V((nb - 1, NCLS, 128), F32),
        V((half0, wt), F32),
        [V((TILES, half0 >> (j + 1), wt), F32) for j in range(nr - 1)],
        [V((TILES, half0 >> j, wt), BF16) for j in range(nr)],
        [V((TILES, half0 >> j, wt), BF16) for j in range(nr)],
        V((TILES, nviews, wt), F32),
        dma((1,)), dma((n_img,)), dma((n_img,)), dma((n_ref,)), dma((n_ref,)),
        dma((nb,)), dma((nb,)), dma((npix + 3,)), dma((npix + 3,)),
        dma((nc, 4)), dma((nc, 4)), dma((4,)), dma((4,)), dma((nc, 4)), dma((nc, 4)),
        dma((nr + 1, TILES)), dma((nr + 1, TILES)), dma((nb - 1,)), dma((nb - 1,)),
        dma((1,)), dma((1,)),
    ]
    return pl.pallas_call(
        functools.partial(kernel, n, m),
        out_shape=(
            jax.ShapeDtypeStruct((nviews, cols), F32),
            jax.ShapeDtypeStruct((rows // m, 128), F32),
            jax.ShapeDtypeStruct((NCLS, 128), F32),
        ),
        in_specs=[vm, hbm, vm, vm],
        out_specs=(vm, vm, vm),
        scratch_shapes=scratch,
        compiler_params=pltpu.CompilerParams(
            collective_id=0, has_side_effects=True, vmem_limit_bytes=62 * 2**20),
    )(images, refs, mask, classes)


def on_device(images, references, cycle_mask, view_class):
    n = lax.axis_size("img")
    m = lax.axis_size("pix")
    c = bit(lax.axis_index("img"), VIEW_BIT)
    nviews = references.shape[0]
    bits = image_bits(n)
    nr = len(bits)
    owner = []
    for slot in range(n // 2):
        at = (slot % 2) * PIXEL_BIT
        for j, b in enumerate(bits):
            at = at + ((slot // 2 ** (nr - j)) % 2) * b
        owner.append(at)
    by_owner = view_class.reshape(n, nviews)
    groups = [
        jnp.concatenate([by_owner[at + g * VIEW_BIT] for at in owner]) for g in range(2)
    ]
    classes = jnp.where(c == 0, groups[0], groups[1])[None, :]
    view_sums, evidence, class_share = whole_step(
        n, m, images, references, cycle_mask[None, :], classes)
    return (view_sums, class_share[:, 0], evidence[:, 0])


def solution(mesh):
    in_specs = (P("img", "pix"), P("img", "pix"), P("pix"), P())
    out_specs = (P("img", "pix"), P(), P(("img", "pix")))
    return jax.shard_map(
        on_device, mesh=mesh, in_specs=in_specs, out_specs=out_specs, check_vma=False
    )
```

time: 1170 us -> 319 us (0.27)
  waiting for transfers between devices: 1050 us -> 0 us
  Pallas kernels: 0 us -> 309 us
  blocking collectives: 47.1 us -> 0 us
  matrix products: 36.9 us -> 0 us
  other arithmetic: 24.9 us -> 0.59 us
  between operations: 13.8 us -> 0.67 us
    reduce_scatter x1 -> x0, waiting for transfers between devices: 654 us -> none  [on_device(): lax.psum_scatter(lax.dot_general(posterior, normed, (((0,), (0,)), ((), (...]
    pallas_call x0 -> x1, Pallas kernels: none -> 309 us  [whole_step(): pl.pallas_call(functools.partial(kernel, n, m), out_shape=(jax.ShapeDtype...]
    all_gather x1 -> x0, waiting for transfers between devices: 265 us -> none  [on_device(): ref_piece = lax.all_gather(references, 'img', axis=0, tiled=True)]
    psum x2 -> x0, waiting for transfers between devices: 125 us -> none  [the longest x1 107 us: on_device(): lax.psum((jnp.sum(widened, 0), jnp.sum(widened * widened, 0)), 'img')]
    psum x2 -> x0, blocking collectives: 47.1 us -> none  [the longest x1 44 us: on_device(): class_total = lax.psum(class_local, 'img')]
    dot_general x3 -> x0, matrix products: 36.9 us -> none  [the longest x1 21.7 us: on_device(): lax.dot_general(posterior, normed, (((0,), (0,)), ((), ())), preferred_el...]
    reduce_sum x6 -> x0, other arithmetic: 21.3 us -> none  [the longest x1 10.3 us: on_device(): ref_energy = jnp.sum(jnp.square(ref_piece.astype(jnp.float32)), 1)]
  transfers between devices with their start and end apart: 4 -> 0, of which waited for: 4 -> 0; matrix products, arithmetic and copies ran while one was open for 1% -> 0% of each run, Pallas kernels for 0% -> 0%
where the time goes in v2:
time: 319 us; the launch traced here: 318 us
  Pallas kernels  309 us (97%)
  local copies, waits for them, and re-layouts  8.02 us (3%)
    pallas_call x1, Pallas kernels, whole_step(): pl.pallas_call(functools.partial(kernel, n, m), out_shape=(jax.ShapeDtype...  309 us

profile of v2, /device:TPU:0, one launch (start us, length us, event | category | flops | bytes accessed | tf_op | source)
XLA Modules:
  0.0 318.2 jit_solution(16853022270812654117)
XLA Ops:
  0.7 1.2 slice_bitcast_fusion
  1.8 0.1 concatenate.69
  1.9 0.1 concatenate.60
  2.0 0.6 broadcast_select_fusion.classes
  2.6 309.0 %shard_map.67 = (f32[96,8192]{1,0:T(8,128)}, f32[128,128]{1,0:T(8,128)}, f32[96,128]{1,0:T(8,128)}) custom-call(bf16[256,8192]{1,0:T(8,128)(2,1)} %images.1, bf16[96,8192]{1,0:T(8,128)(2,1)} %refs.1, s32[1,8192]{1,0:T(1,128)} %bitcast.33, s32[1,768]{1,0:T(1,128)} %broadcast_select_fusion.classes), custom_call_target="tpu_custom_call" | custom-call | tf_op jit(solution)/shard_map/pallas_call | solution.py:527
  311.6 1.4 slice_reduce_fusion.1
  313.0 1.5 slice_reduce_fusion
  314.5 3.8 %copy.8 = f32[96,8192]{1,0:T(8,128)} copy(f32[96,8192]{1,0:T(8,128)} %get-tuple-element.28) | data formatting | bytes 6291456

commit v3 on v2

--- a/solution.py
+++ b/solution.py
@@ -17,7 +17,6 @@
 PIXEL_BIT = 4
 VIEW_BIT = 2
 CHUNKS = 4
-TILES = 8
 
 
 def image_bits(n):
@@ -28,6 +27,10 @@
     return [2**j for j in range(20) if 2**j < m]
 
 
+def pixel_tiles(q):
+    return min(16, q // 128)
+
+
 def bit(index, value):
     return (index // value) % 2
 
@@ -42,7 +45,7 @@
 
 def kernel(n, m, images, refs, mask, classes, out, ev_out, cls_out,
            img_all, pair_img, ref_all, stat, stat_in, col, bg, bg_mine, bg_in,
-           ecol, erow, partial, halves, soft, soft_in, evb, post, post_t,
+           ecol, erow, partial, halves, soft, soft_in, evb, ev_all, post, post_t,
            mass, mass_in, fresh, keep, sends, recvs, last,
            lsem, isend, irecv, rsend, rrecv, tsend, trecv, bsend, brecv,
            hsend, hrecv, csend, crecv, gsend, grecv, vsend, vrecv, ksend, krecv,
@@ -112,9 +115,19 @@
     order = list(reversed(list(zip(bits, weights))))
     pair_ref = send_ref(refs.at[:, theirs], slot, kp)
     stage = [[] for _ in order]
-    for j, (b, w) in enumerate(order):
-        stage[j].append((send_ref(refs.at[:, mine], slot, flip(d, b)), slot))
-    img_across = send_img(images.at[:, mine], img_all.at[own], cp)
+
+    def spread(src, s, first, stop):
+        for j in range(first, stop):
+            stage[j].append((send_ref(src, s, flip(d, order[j][0])), s))
+
+    far = len(order) - 1
+    spread(refs.at[:, mine], slot, far, far + 1)
+    img_across = []
+
+    def send_across(i):
+        img_across.append(send_img(images.at[chunk(i), mine], img_all.at[own, chunk(i)], cp))
+
+    send_across(0)
     own_ref = pltpu.make_async_copy(refs.at[:, mine], ref_all.at[slot], lsem.at[0])
     own_ref.start()
 
@@ -128,26 +141,37 @@
         return 0
 
     lax.fori_loop(0, cols // wide, col_tile, 0)
-    img_k = []
-    hops = [*bits, VIEW_BIT, PIXEL_BIT]
-    for j, b in enumerate(hops):
-        x = remote(stat.at[j], stat_in.at[j], tsend.at[j], trecv.at[j], "img", flip(d, b))
+    hops = [PIXEL_BIT, *[b for b, _ in order[:-1]], VIEW_BIT, order[-1][0]]
+
+    def hop(j):
+        x = remote(stat.at[j], stat_in.at[j], tsend.at[j], trecv.at[j], "img", flip(d, hops[j]))
         x.start()
         x.wait()
         stat[j + 1] = stat[j] + stat_in[j]
-        if j == 1:
-            img_k.append(send_img(images.at[chunk(0), theirs], pair_img.at[chunk(0)], kp))
+
+    img_k = []
+
+    def send_pair(i):
+        img_k.append(send_img(images.at[chunk(i), theirs], pair_img.at[chunk(i)], kp))
+
+    for j in range(len(order)):
+        hop(j)
+    spread(refs.at[:, mine], slot, 0, far)
+    arrive(pair_ref)
+    pair_slot = slot + 1 - 2 * k
+    spread(ref_all.at[pair_slot], pair_slot, 0, far)
+    for i in range(CHUNKS - 1):
+        send_pair(i)
+    for j in range(len(order), len(hops)):
+        hop(j)
+    for i in range(1, CHUNKS):
+        send_across(i)
+    spread(ref_all.at[pair_slot], pair_slot, far, far + 1)
     total = rows * n
     nh = len(hops)
     col_mean = stat[nh, 0:1, :] / total
     col[0:1, :] = col_mean
     col[1:2, :] = 1.0 / jnp.sqrt(stat[nh, 1:2, :] / total - col_mean * col_mean + EPSILON)
-
-    arrive(pair_ref)
-    pair_slot = slot + 1 - 2 * k
-    for j, (b, w) in enumerate(order):
-        stage[j].append((send_ref(ref_all.at[pair_slot], pair_slot, flip(d, b)), pair_slot))
-    img_k.append(send_img(images.at[chunk(1), theirs], pair_img.at[chunk(1)], kp))
 
     def bg_tile(t, carry):
         s, sq, cnt = carry
@@ -182,21 +206,20 @@
     bg[own] = jnp.where(lane == 0, bg_mean, bg_inv)
     bg_k = remote(bg.at[own], bg.at[own], bsend.at[np_], brecv.at[np_], "img", kp)
     bg_k.start()
+    send_pair(CHUNKS - 1)
     bg_c = remote(bg.at[own], bg.at[own], bsend.at[np_ + 1], brecv.at[np_ + 1], "img", cp)
     bg_c.start()
 
     ncol = min(512, q)
 
-    def normalise(read, s):
+    def normalise(read, s, r=pl.ds(0, rows)):
         def tile(t, _):
             at = aligned(t * ncol, ncol, 128)
             there = aligned(k * q + t * ncol, ncol, 128)
-            w = (read(t, at, there).astype(F32) - col[0:1, there]) * col[1:2, there]
-            img_all[s, :, at] = ((w - bg[s, :, 0:1]) * bg[s, :, 1:2]).astype(BF16)
+            w = (read(at, there).astype(F32) - col[0:1, there]) * col[1:2, there]
+            img_all[s, r, at] = ((w - bg[s, r, 0:1]) * bg[s, r, 1:2]).astype(BF16)
             return 0
         lax.fori_loop(0, q // ncol, tile, 0)
-
-    normalise(lambda t, at, there: images[:, there], own)
 
     def energy(s):
         def tile(t, acc):
@@ -208,40 +231,33 @@
         acc = lax.fori_loop(0, q // ncol, tile, jnp.zeros((nviews, 128), F32))
         ecol[s] = jnp.broadcast_to(jnp.sum(acc, 1, keepdims=True), (nviews, 128))
 
-    bg_k.wait_recv()
-    bg_d = remote(bg.at[other], bg.at[other], bsend.at[np_ + 2], brecv.at[np_ + 2], "img", cp)
-    bg_d.start()
-
-    sent_k = [2]
-
-    def next_k():
-        i = sent_k[0]
-        if i < CHUNKS:
-            img_k.append(send_img(images.at[chunk(i), theirs], pair_img.at[chunk(i)], kp))
-            sent_k[0] += 1
-
-    fwd = []
-
-    def forward_img():
-        i = len(fwd)
-        if i < CHUNKS:
-            arrive(img_k[i])
-            fwd.append(send_img(pair_img.at[chunk(i)], img_all.at[other, chunk(i)], cp))
-            next_k()
-
     for j, (b, w) in enumerate(order[:-1]):
         for x, s in stage[j]:
             arrive(x)
             got = s + w * (1 - 2 * bit(d, b))
-            for j2 in range(j + 1, len(order)):
-                stage[j2].append((send_ref(ref_all.at[got], got, flip(d, order[j2][0])), got))
-            forward_img()
-    while len(fwd) < CHUNKS:
-        forward_img()
-    normalise(lambda t, at, there: pair_img[:, at], other)
-    own_ref.wait()
-    energy(slot)
-    energy(pair_slot)
+            spread(ref_all.at[got], got, j + 1, len(order))
+            if len(stage[0]) and x is stage[0][0][0]:
+                normalise(lambda at, there: images[:, there], own)
+                own_ref.wait()
+                energy(slot)
+                energy(pair_slot)
+    bg_k.wait_recv()
+    bg_d = remote(bg.at[other], bg.at[other], bsend.at[np_ + 2], brecv.at[np_ + 2], "img", cp)
+    bg_d.start()
+
+    fwd = []
+
+    def forward_img(i):
+        arrive(img_k[i])
+        fwd.append(send_img(pair_img.at[chunk(i)], img_all.at[other, chunk(i)], cp))
+        normalise(lambda at, there: pair_img[chunk(i), at], other, chunk(i))
+
+    forward_img(0)
+    bg_c.wait_recv()
+    for x in img_across:
+        arrive(x)
+    normalise(lambda at, there: img_all[across, :, at], across)
+    forward_img(1)
     for j, (b, w) in enumerate(order):
         for x, s in stage[j]:
             arrive(x)
@@ -279,22 +295,15 @@
         held = aligned(starts[j + 1], sizes[j + 1], sizes[j + 1])
         partial[s, held, :] += halves[j][s]
 
-    def slot_of(i):
-        return 2 * ((c + i // 2) % 2) + i % 2
-
-    def begin(i, _):
-        s = slot_of(i)
+    def begin(s):
         score(s)
         halve(0, s).start()
-        return 0
-
-    def middle(j):
-        def body(i, _):
-            s = slot_of(i)
-            absorb_half(j, s)
-            halve(j + 1, s).start()
-            return 0
-        return body
+
+    def middle(*slots):
+        for j in range(nc - 1):
+            for s in slots:
+                absorb_half(j, s)
+                halve(j + 1, s).start()
 
     nlast = sizes[-1]
     held = aligned(starts[-1], nlast, nlast)
@@ -303,8 +312,7 @@
     def soft_copy(s):
         return remote(soft.at[s], soft_in.at[s], csend.at[s], crecv.at[s], "img", cp)
 
-    def soften(i, _):
-        s = slot_of(i)
+    def soften(s):
         absorb_half(nc - 1, s)
         x = partial[s, held, :] * (4.0 / SIDE)
         partial[s, held, :] = x
@@ -314,15 +322,13 @@
             jnp.where(lane2 == 1, jnp.sum(jnp.exp(x - top), 1, keepdims=True),
                       jnp.sum(x, 1, keepdims=True)))
         soft_copy(s).start()
-        return 0
 
     def grow(j, s):
         axis, b, partner, mybit = cuts[j]
         at = aligned(starts[j + 1], sizes[j + 1], sizes[j + 1])
         return remote(post.at[s, at], post.at[s, at], gsend.at[j, s], grecv.at[j, s], axis, partner)
 
-    def settle(i, _):
-        s = slot_of(i)
+    def settle(s):
         soft_copy(s).wait_recv()
         a, b = soft[s], soft_in[s]
         top = jnp.maximum(a[:, 0:1], b[:, 0:1])
@@ -332,47 +338,51 @@
             log_total - (a[:, 2:3] + b[:, 2:3]) / (nviews * n), (nlast, 128))
         post[s, held, :] = jnp.exp(partial[s, held, :] - log_total).astype(BF16)
         grow(nc - 1, s).start()
-        return 0
-
-    lax.fori_loop(0, 2, begin, 0)
-    for j in range(nc - 1):
-        lax.fori_loop(0, 2, middle(j), 0)
-    bg_c.wait_recv()
-    arrive(img_across)
-    normalise(lambda t, at, there: img_all[across, :, at], across)
+
+    begin(own)
+    begin(across)
+    for i in range(2, CHUNKS - 1):
+        forward_img(i)
+    middle(own, across)
+    forward_img(CHUNKS - 1)
+    begin(other)
     bg_d.wait_recv()
-    for x in fwd:
-        arrive(x)
-    normalise(lambda t, at, there: img_all[diag, :, at], diag)
-    lax.fori_loop(2, 4, begin, 0)
-    lax.fori_loop(0, 2, soften, 0)
-    for j in range(nc - 1):
-        lax.fori_loop(2, 4, middle(j), 0)
-    lax.fori_loop(2, 4, soften, 0)
-    lax.fori_loop(0, 4, settle, 0)
+
+    def take_diag(i):
+        arrive(fwd[i])
+        normalise(lambda at, there: img_all[diag, chunk(i), at], diag, chunk(i))
+
+    for i in range(CHUNKS - 1):
+        take_diag(i)
+    middle(other)
+    take_diag(CHUNKS - 1)
+    begin(diag)
+    soften(other)
+    soften(own)
+    middle(diag)
+    soften(diag)
+    soften(across)
+    turns = [diag, across, other, own]
+    for s in turns:
+        settle(s)
     for j in range(nc - 1, 0, -1):
-        def grown(i, _, j=j):
-            s = slot_of(i)
+        for s in turns:
             grow(j, s).wait_recv()
             grow(j - 1, s).start()
-            return 0
-        lax.fori_loop(0, 4, grown, 0)
 
     half0 = nv // 2
-
-    def turn(i, acc):
-        s = slot_of(i)
+    class_mass = jnp.zeros((1, nv), F32)
+    for s in turns:
         grow(0, s).wait_recv()
         x = post[s].astype(F32)
         xt = jnp.transpose(x).astype(BF16)
         at = aligned(s * rows, rows, 128)
         post_t[0, :, at] = xt[:half0]
         post_t[1, :, at] = xt[half0:]
-        return acc + jnp.sum(x, 0, keepdims=True)
-
-    class_mass = lax.fori_loop(0, 4, turn, jnp.zeros((1, nv), F32))
-
-    wt = q // TILES
+        class_mass = class_mass + jnp.sum(x, 0, keepdims=True)
+
+    tiles = pixel_tiles(q)
+    wt = q // tiles
     partners = [flip(d, b) for b in bits]
     mybits = [bit(d, b) for b in bits] + [k]
 
@@ -396,10 +406,10 @@
         stage_copy(0, t).start()
         return 0
 
-    lax.fori_loop(0, TILES, first, 0)
-
-    ev_out[aligned(k * nlast, nlast, nlast), :] = evb[own]
-    ev_copy = remote(evb.at[other], ev_out.at[aligned(k * nlast, nlast, nlast)],
+    lax.fori_loop(0, tiles, first, 0)
+
+    ev_all[aligned(k * nlast, nlast, nlast), :] = evb[own]
+    ev_copy = remote(evb.at[other], ev_all.at[aligned(k * nlast, nlast, nlast)],
                      esend.at[0], erecv.at[0], "img", kp)
     ev_copy.start()
 
@@ -450,22 +460,23 @@
     def ramp(ts):
         for t in ts:
             for j in range(nr):
-                if 0 <= t - j < TILES:
+                if 0 <= t - j < tiles:
                     absorb(j, t - j)
 
     ramp(range(nr - 1))
     mass_hop(0)
-    lax.fori_loop(nr - 1, TILES // 2, lambda t, _: (steps(t), 0)[1], 0)
+    lax.fori_loop(nr - 1, tiles // 2, lambda t, _: (steps(t), 0)[1], 0)
     mass_hop(1)
-    lax.fori_loop(TILES // 2, TILES, lambda t, _: (steps(t), 0)[1], 0)
+    lax.fori_loop(tiles // 2, tiles, lambda t, _: (steps(t), 0)[1], 0)
     for j in range(2, len(mass_hops)):
         mass_hop(j)
-    cls_out[...] = mass[len(mass_hops)] * (NCLS / total)
-    ramp(range(TILES, TILES + nr - 1))
+    cls_out[...] = jnp.transpose(mass[len(mass_hops)] * (NCLS / total))[0:1]
+    ramp(range(tiles, tiles + nr - 1))
 
     for x in ref_copies + img_copies + [bg_k, bg_c, bg_d]:
         x.wait_send()
     ev_copy.wait()
+    ev_out[...] = jnp.transpose(ev_all[...])[0:1]
 
     def drain(s, _):
         soft_copy(s).wait_send()
@@ -482,7 +493,7 @@
             stage_copy(j, t).wait_send()
         return 0
 
-    lax.fori_loop(0, TILES, finish, 0)
+    lax.fori_loop(0, tiles, finish, 0)
 
 
 def whole_step(n, m, images, refs, mask, classes):
@@ -496,10 +507,11 @@
     nc = npix + 1
     nv = nviews * n // 2
     half0 = nv // 2
-    wt = q // TILES
+    tiles = pixel_tiles(q)
+    wt = q // tiles
     nlast = rows >> nc
     n_ref = 1 + sum(2 ** (j + 1) for j in range(nr))
-    n_img = 1 + 2 * CHUNKS
+    n_img = 3 * CHUNKS
     vm = pl.BlockSpec(memory_space=pltpu.VMEM)
     hbm = pl.BlockSpec(memory_space=pl.ANY)
     V = pltpu.VMEM
@@ -511,25 +523,26 @@
         V((n // 2, nviews, 128), F32), V((8, nv), F32),
         V((4, rows, nv), F32), [V((4, rows >> (j + 1), nv), F32) for j in range(nc)],
         V((4, nlast, 128), F32), V((4, nlast, 128), F32), V((4, nlast, 128), F32),
+        V((rows // m, 128), F32),
         V((4, rows, nv), BF16), V((2, half0, 4 * rows), BF16),
         V((nb, NCLS, 128), F32), V((nb - 1, NCLS, 128), F32),
         V((half0, wt), F32),
-        [V((TILES, half0 >> (j + 1), wt), F32) for j in range(nr - 1)],
-        [V((TILES, half0 >> j, wt), BF16) for j in range(nr)],
-        [V((TILES, half0 >> j, wt), BF16) for j in range(nr)],
-        V((TILES, nviews, wt), F32),
+        [V((tiles, half0 >> (j + 1), wt), F32) for j in range(nr - 1)],
+        [V((tiles, half0 >> j, wt), BF16) for j in range(nr)],
+        [V((tiles, half0 >> j, wt), BF16) for j in range(nr)],
+        V((tiles, nviews, wt), F32),
         dma((1,)), dma((n_img,)), dma((n_img,)), dma((n_ref,)), dma((n_ref,)),
         dma((nb,)), dma((nb,)), dma((npix + 3,)), dma((npix + 3,)),
         dma((nc, 4)), dma((nc, 4)), dma((4,)), dma((4,)), dma((nc, 4)), dma((nc, 4)),
-        dma((nr + 1, TILES)), dma((nr + 1, TILES)), dma((nb - 1,)), dma((nb - 1,)),
+        dma((nr + 1, tiles)), dma((nr + 1, tiles)), dma((nb - 1,)), dma((nb - 1,)),
         dma((1,)), dma((1,)),
     ]
     return pl.pallas_call(
         functools.partial(kernel, n, m),
         out_shape=(
             jax.ShapeDtypeStruct((nviews, cols), F32),
-            jax.ShapeDtypeStruct((rows // m, 128), F32),
-            jax.ShapeDtypeStruct((NCLS, 128), F32),
+            jax.ShapeDtypeStruct((1, rows // m), F32),
+            jax.ShapeDtypeStruct((1, NCLS), F32),
         ),
         in_specs=[vm, hbm, vm, vm],
         out_specs=(vm, vm, vm),
@@ -559,7 +572,7 @@
     classes = jnp.where(c == 0, groups[0], groups[1])[None, :]
     view_sums, evidence, class_share = whole_step(
         n, m, images, references, cycle_mask[None, :], classes)
-    return (view_sums, class_share[:, 0], evidence[:, 0])
+    return (view_sums, class_share[0], evidence[0])
 
 
 def solution(mesh):

time: 319 us -> 327 us (1.025)
  Pallas kernels: 309 us -> 319 us
    pallas_call x1, Pallas kernels: 309 us -> 319 us  [whole_step(): pl.pallas_call(functools.partial(kernel, n, m), out_shape=(jax.ShapeDtype...]
where the time goes in v3:
time: 327 us
  Pallas kernels  319 us (98%)
  local copies, waits for them, and re-layouts  6.16 us (2%)
    pallas_call x1, Pallas kernels, whole_step(): pl.pallas_call(functools.partial(kernel, n, m), out_shape=(jax.ShapeDtype...  319 us

profile of v3, /device:TPU:0, one launch (start us, length us, event | category | flops | bytes accessed | tf_op | source)
XLA Modules:
  0.0 326.6 jit_solution(16333557179172619397)
XLA Ops:
  0.7 1.2 slice_bitcast_fusion
  1.8 0.1 concatenate.69
  1.9 0.1 concatenate.60
  2.0 0.6 broadcast_select_fusion.classes
  2.6 319.2 %shard_map.67 = (f32[96,8192]{1,0:T(8,128)}, f32[1,128]{1,0:T(1,128)}, f32[1,96]{1,0:T(1,128)}) custom-call(bf16[256,8192]{1,0:T(8,128)(2,1)} %images.1, bf16[96,8192]{1,0:T(8,128)(2,1)} %refs.1, s32[1,8192]{1,0:T(1,128)} %bitcast.35, s32[1,768]{1,0:T(1,128)} %broadcast_select_fusion.classes), custom_call_target="tpu_custom_call" | custom-call | tf_op jit(solution)/shard_map/pallas_call | solution.py:540
  321.8 0.0 copy-start.1
  321.8 0.0 copy-start
  321.8 3.8 %copy.10 = f32[96,8192]{1,0:T(8,128)} copy(f32[96,8192]{1,0:T(8,128)} %get-tuple-element.28) | data formatting | bytes 6291456
  325.6 0.0 copy-done.1
  325.6 0.5 copy.11
  326.1 0.0 copy-done
  326.1 0.5 copy.12
Async XLA Ops:
  321.8 3.8 %copy-start.1 = (f32[1,96]{1,0:T(1,128)S(1)}, f32[1,96]{1,0:T(1,128)}, u32[]{:S(2)}) copy-start(f32[1,96]{1,0:T(1,128)} %get-tuple-element.7) | copy-start | bytes 1156
  321.8 4.3 %copy-start = (f32[1,128]{1,0:T(1,128)S(1)}, f32[1,128]{1,0:T(1,128)}, u32[]{:S(2)}) copy-start(f32[1,128]{1,0:T(1,128)} %get-tuple-element.8) | copy-start | bytes 1540

commit v4 on v3

--- a/solution.py
+++ b/solution.py
@@ -113,7 +113,6 @@
         return pl.ds(i * step, step)
 
     order = list(reversed(list(zip(bits, weights))))
-    pair_ref = send_ref(refs.at[:, theirs], slot, kp)
     stage = [[] for _ in order]
 
     def spread(src, s, first, stop):
@@ -127,7 +126,13 @@
     def send_across(i):
         img_across.append(send_img(images.at[chunk(i), mine], img_all.at[own, chunk(i)], cp))
 
+    img_k = []
+
+    def send_pair(i):
+        img_k.append(send_img(images.at[chunk(i), theirs], pair_img.at[chunk(i)], kp))
+
     send_across(0)
+    send_pair(0)
     own_ref = pltpu.make_async_copy(refs.at[:, mine], ref_all.at[slot], lsem.at[0])
     own_ref.start()
 
@@ -149,24 +154,13 @@
         x.wait()
         stat[j + 1] = stat[j] + stat_in[j]
 
-    img_k = []
-
-    def send_pair(i):
-        img_k.append(send_img(images.at[chunk(i), theirs], pair_img.at[chunk(i)], kp))
-
     for j in range(len(order)):
         hop(j)
+    pair_ref = send_ref(refs.at[:, theirs], slot, kp)
     spread(refs.at[:, mine], slot, 0, far)
-    arrive(pair_ref)
-    pair_slot = slot + 1 - 2 * k
-    spread(ref_all.at[pair_slot], pair_slot, 0, far)
-    for i in range(CHUNKS - 1):
-        send_pair(i)
-    for j in range(len(order), len(hops)):
-        hop(j)
-    for i in range(1, CHUNKS):
-        send_across(i)
-    spread(ref_all.at[pair_slot], pair_slot, far, far + 1)
+    hop(len(order))
+    send_across(1)
+    hop(len(order) + 1)
     total = rows * n
     nh = len(hops)
     col_mean = stat[nh, 0:1, :] / total
@@ -206,7 +200,6 @@
     bg[own] = jnp.where(lane == 0, bg_mean, bg_inv)
     bg_k = remote(bg.at[own], bg.at[own], bsend.at[np_], brecv.at[np_], "img", kp)
     bg_k.start()
-    send_pair(CHUNKS - 1)
     bg_c = remote(bg.at[own], bg.at[own], bsend.at[np_ + 1], brecv.at[np_ + 1], "img", cp)
     bg_c.start()
 
@@ -231,37 +224,50 @@
         acc = lax.fori_loop(0, q // ncol, tile, jnp.zeros((nviews, 128), F32))
         ecol[s] = jnp.broadcast_to(jnp.sum(acc, 1, keepdims=True), (nviews, 128))
 
+    fwd = []
+
+    def forward_img(i):
+        arrive(img_k[i])
+        fwd.append(send_img(pair_img.at[chunk(i)], img_all.at[other, chunk(i)], cp))
+
+    def take_pair(i):
+        normalise(lambda at, there: pair_img[chunk(i), at], other, chunk(i))
+
+    for i in range(2, CHUNKS):
+        send_across(i)
+    forward_img(0)
+    arrive(pair_ref)
+    pair_slot = slot + 1 - 2 * k
+    spread(ref_all.at[pair_slot], pair_slot, 0, far)
+    for i in range(1, CHUNKS):
+        send_pair(i)
+    spread(ref_all.at[pair_slot], pair_slot, far, far + 1)
+    normalise(lambda at, there: images[:, there], own)
+    own_ref.wait()
+    energy(slot)
+    energy(pair_slot)
+    bg_k.wait_recv()
+    bg_d = remote(bg.at[other], bg.at[other], bsend.at[np_ + 2], brecv.at[np_ + 2], "img", cp)
+    bg_d.start()
+    ready = 0
     for j, (b, w) in enumerate(order[:-1]):
         for x, s in stage[j]:
             arrive(x)
             got = s + w * (1 - 2 * bit(d, b))
             spread(ref_all.at[got], got, j + 1, len(order))
-            if len(stage[0]) and x is stage[0][0][0]:
-                normalise(lambda at, there: images[:, there], own)
-                own_ref.wait()
-                energy(slot)
-                energy(pair_slot)
-    bg_k.wait_recv()
-    bg_d = remote(bg.at[other], bg.at[other], bsend.at[np_ + 2], brecv.at[np_ + 2], "img", cp)
-    bg_d.start()
-
-    fwd = []
-
-    def forward_img(i):
-        arrive(img_k[i])
-        fwd.append(send_img(pair_img.at[chunk(i)], img_all.at[other, chunk(i)], cp))
-        normalise(lambda at, there: pair_img[chunk(i), at], other, chunk(i))
-
-    forward_img(0)
-    bg_c.wait_recv()
-    for x in img_across:
+            energy(got)
+            if ready == 0:
+                take_pair(0)
+                bg_c.wait_recv()
+                for y in img_across:
+                    arrive(y)
+                normalise(lambda at, there: img_all[across, :, at], across)
+            ready += 1
+    forward_img(1)
+    take_pair(1)
+    for x, s in stage[far]:
         arrive(x)
-    normalise(lambda at, there: img_all[across, :, at], across)
-    forward_img(1)
-    for j, (b, w) in enumerate(order):
-        for x, s in stage[j]:
-            arrive(x)
-            energy(s + w * (1 - 2 * bit(d, b)))
+        energy(s + order[far][1] * (1 - 2 * bit(d, order[far][0])))
     erow[...] = jnp.transpose(ecol[...].reshape(-1, 128))[0:8]
 
     nv = nviews * n // 2
@@ -339,12 +345,14 @@
         post[s, held, :] = jnp.exp(partial[s, held, :] - log_total).astype(BF16)
         grow(nc - 1, s).start()
 
+    for i in range(2, CHUNKS - 1):
+        forward_img(i)
+        take_pair(i)
     begin(own)
     begin(across)
-    for i in range(2, CHUNKS - 1):
-        forward_img(i)
+    forward_img(CHUNKS - 1)
+    take_pair(CHUNKS - 1)
     middle(own, across)
-    forward_img(CHUNKS - 1)
     begin(other)
     bg_d.wait_recv()
 
@@ -401,34 +409,34 @@
         place = aligned(k * q + t * wt, wt, 128)
         return remote(last.at[t], out.at[:, place], vsend.at[nr, t], vrecv.at[nr, t], "img", kp)
 
+    hit = lax.broadcasted_iota(jnp.int32, (NCLS, nv), 0) == classes[...]
+    mass[0] = jnp.broadcast_to(
+        jnp.sum(jnp.where(hit, class_mass, 0.0), 1, keepdims=True), (NCLS, 128))
+    mass_hops = [*bits, VIEW_BIT]
+
+    def mass_copy(j):
+        return remote(mass.at[j], mass_in.at[j], ksend.at[j], krecv.at[j], "img", flip(d, mass_hops[j]))
+
+    def mass_hop(j):
+        mass_copy(j).wait()
+        mass[j + 1] = mass[j] + mass_in[j]
+        if j + 1 < len(mass_hops):
+            mass_copy(j + 1).start()
+
+    mass_copy(0).start()
+
+    ev_all[aligned(k * nlast, nlast, nlast), :] = evb[own]
+    ev_copy = remote(evb.at[other], ev_all.at[aligned(k * nlast, nlast, nlast)],
+                     esend.at[0], erecv.at[0], "img", kp)
+    ev_copy.start()
+
     def first(t, _):
         sends[0][t] = weigh(1 - mybits[0], t).astype(BF16)
         stage_copy(0, t).start()
         return 0
 
     lax.fori_loop(0, tiles, first, 0)
-
-    ev_all[aligned(k * nlast, nlast, nlast), :] = evb[own]
-    ev_copy = remote(evb.at[other], ev_all.at[aligned(k * nlast, nlast, nlast)],
-                     esend.at[0], erecv.at[0], "img", kp)
-    ev_copy.start()
-
-    hit = lax.broadcasted_iota(jnp.int32, (NCLS, nv), 0) == classes[...]
-    mass[0] = jnp.broadcast_to(
-        jnp.sum(jnp.where(hit, class_mass, 0.0), 1, keepdims=True), (NCLS, 128))
-    mass_hops = [*bits, VIEW_BIT]
-
-    def mass_copy(j):
-        return remote(mass.at[j], mass_in.at[j], ksend.at[j], krecv.at[j], "img", flip(d, mass_hops[j]))
-
-    mass_copy(0).start()
-
-    def mass_hop(j):
-        if j < len(mass_hops):
-            mass_copy(j).wait()
-            mass[j + 1] = mass[j] + mass_in[j]
-            if j + 1 < len(mass_hops):
-                mass_copy(j + 1).start()
+    mass_hop(0)
 
     def absorb(j, t):
         size = half0 >> (j + 1)
@@ -464,14 +472,12 @@
                     absorb(j, t - j)
 
     ramp(range(nr - 1))
-    mass_hop(0)
-    lax.fori_loop(nr - 1, tiles // 2, lambda t, _: (steps(t), 0)[1], 0)
+    lax.fori_loop(nr - 1, tiles, lambda t, _: (steps(t), 0)[1], 0)
     mass_hop(1)
-    lax.fori_loop(tiles // 2, tiles, lambda t, _: (steps(t), 0)[1], 0)
+    ramp(range(tiles, tiles + nr - 1))
     for j in range(2, len(mass_hops)):
         mass_hop(j)
     cls_out[...] = jnp.transpose(mass[len(mass_hops)] * (NCLS / total))[0:1]
-    ramp(range(tiles, tiles + nr - 1))
 
     for x in ref_copies + img_copies + [bg_k, bg_c, bg_d]:
         x.wait_send()

time: 327 us -> 249 us (0.76)
  Pallas kernels: 319 us -> 241 us
    pallas_call x1, Pallas kernels: 319 us -> 241 us  [whole_step(): pl.pallas_call(functools.partial(kernel, n, m), out_shape=(jax.ShapeDtype...]
where the time goes in v4:
time: 249 us
  Pallas kernels  241 us (97%)
  local copies, waits for them, and re-layouts  6.16 us (2%)
    pallas_call x1, Pallas kernels, whole_step(): pl.pallas_call(functools.partial(kernel, n, m), out_shape=(jax.ShapeDtype...  241 us

profile of v4, /device:TPU:0, one launch (start us, length us, event | category | flops | bytes accessed | tf_op | source)
XLA Modules:
  0.0 248.7 jit_solution(1266154479132183954)
XLA Ops:
  0.7 1.2 slice_bitcast_fusion
  1.8 0.1 concatenate.69
  1.9 0.1 concatenate.60
  2.0 0.6 broadcast_select_fusion.classes
  2.6 241.3 %shard_map.67 = (f32[96,8192]{1,0:T(8,128)}, f32[1,128]{1,0:T(1,128)}, f32[1,96]{1,0:T(1,128)}) custom-call(bf16[256,8192]{1,0:T(8,128)(2,1)} %images.1, bf16[96,8192]{1,0:T(8,128)(2,1)} %refs.1, s32[1,8192]{1,0:T(1,128)} %bitcast.35, s32[1,768]{1,0:T(1,128)} %broadcast_select_fusion.classes), custom_call_target="tpu_custom_call" | custom-call | tf_op jit(solution)/shard_map/pallas_call | solution.py:546
  243.9 0.0 copy-start.1
  243.9 0.0 copy-start
  244.0 3.8 %copy.10 = f32[96,8192]{1,0:T(8,128)} copy(f32[96,8192]{1,0:T(8,128)} %get-tuple-element.28) | data formatting | bytes 6291456
  247.7 0.0 copy-done.1
  247.7 0.5 copy.11
  248.2 0.0 copy-done
  248.2 0.5 copy.12
Async XLA Ops:
  243.9 3.8 %copy-start.1 = (f32[1,96]{1,0:T(1,128)S(1)}, f32[1,96]{1,0:T(1,128)}, u32[]{:S(2)}) copy-start(f32[1,96]{1,0:T(1,128)} %get-tuple-element.7) | copy-start | bytes 1156
  243.9 4.3 %copy-start = (f32[1,128]{1,0:T(1,128)S(1)}, f32[1,128]{1,0:T(1,128)}, u32[]{:S(2)}) copy-start(f32[1,128]{1,0:T(1,128)} %get-tuple-element.8) | copy-start | bytes 1540

commit v5 on v4

--- a/solution.py
+++ b/solution.py
@@ -16,7 +16,7 @@
 
 PIXEL_BIT = 4
 VIEW_BIT = 2
-CHUNKS = 4
+CHUNKS = 8
 
 
 def image_bits(n):
@@ -348,8 +348,10 @@
     for i in range(2, CHUNKS - 1):
         forward_img(i)
         take_pair(i)
-    begin(own)
-    begin(across)
+        if i == CHUNKS // 2:
+            begin(own)
+        if i == CHUNKS // 2 + 1:
+            begin(across)
     forward_img(CHUNKS - 1)
     take_pair(CHUNKS - 1)
     middle(own, across)

time: 249 us -> 255 us (1.024)
  Pallas kernels: 241 us -> 248 us
    pallas_call x1, Pallas kernels: 241 us -> 248 us  [whole_step(): pl.pallas_call(functools.partial(kernel, n, m), out_shape=(jax.ShapeDtype...]
where the time goes in v5:
time: 255 us
  Pallas kernels  248 us (97%)
  local copies, waits for them, and re-layouts  6.16 us (2%)
    pallas_call x1, Pallas kernels, whole_step(): pl.pallas_call(functools.partial(kernel, n, m), out_shape=(jax.ShapeDtype...  248 us

profile of v5, /device:TPU:0, one launch (start us, length us, event | category | flops | bytes accessed | tf_op | source)
XLA Modules:
  0.0 255.1 jit_solution(2667352480784893567)
XLA Ops:
  0.7 1.2 slice_bitcast_fusion
  1.8 0.1 concatenate.69
  1.9 0.1 concatenate.60
  2.0 0.6 broadcast_select_fusion.classes
  2.6 247.6 %shard_map.67 = (f32[96,8192]{1,0:T(8,128)}, f32[1,128]{1,0:T(1,128)}, f32[1,96]{1,0:T(1,128)}) custom-call(bf16[256,8192]{1,0:T(8,128)(2,1)} %images.1, bf16[96,8192]{1,0:T(8,128)(2,1)} %refs.1, s32[1,8192]{1,0:T(1,128)} %bitcast.35, s32[1,768]{1,0:T(1,128)} %broadcast_select_fusion.classes), custom_call_target="tpu_custom_call" | custom-call | tf_op jit(solution)/shard_map/pallas_call | solution.py:548
  250.3 0.0 copy-start.1
  250.3 0.0 copy-start
  250.3 3.8 %copy.10 = f32[96,8192]{1,0:T(8,128)} copy(f32[96,8192]{1,0:T(8,128)} %get-tuple-element.28) | data formatting | bytes 6291456
  254.1 0.0 copy-done.1
  254.1 0.5 copy.11
  254.6 0.0 copy-done
  254.6 0.5 copy.12
Async XLA Ops:
  250.3 3.8 %copy-start.1 = (f32[1,96]{1,0:T(1,128)S(1)}, f32[1,96]{1,0:T(1,128)}, u32[]{:S(2)}) copy-start(f32[1,96]{1,0:T(1,128)} %get-tuple-element.7) | copy-start | bytes 1156
  250.3 4.3 %copy-start = (f32[1,128]{1,0:T(1,128)S(1)}, f32[1,128]{1,0:T(1,128)}, u32[]{:S(2)}) copy-start(f32[1,128]{1,0:T(1,128)} %get-tuple-element.8) | copy-start | bytes 1540
